TPU v7x, 32 devices: a whole 2x2x4 slice. The times are simulated.
32 devices in a mesh: groups: 2 (over x), dates: 16 (over z, y, core).
Axes of the slice: x: 2, y: 2, z: 4, core: 2. Of those that a mesh axis runs over, the one named last changes fastest.
Arguments:
- scenes: bfloat16 [64, 16, 7, 256], P(('groups', 'dates')), parts along dimension 0, as said below
- quality: bfloat16 [64, 16, 256], P(('groups', 'dates')), parts along dimension 0, may hold values from 0.099609375 to 1
- pif_mask: float32 [32, 256], P(('groups', 'dates')), parts along dimension 0, may hold values from 0.05 to 1
- counts: int32 [32], P(('groups', 'dates')), parts along dimension 0, may hold values from 1 to 32, as said below
Outputs:
- normalized: bfloat16 [64, 16, 7, 256], P(('groups', 'dates')), parts along dimension 0
There are 2 independent parts, one for each index of `groups`. A program takes and returns all parts, laid end to end along the dimension named above; each array names one. Nothing has to cross between parts.
Inputs may be any that keep to these rules, and one draw needn't show every extreme that they name: Tile t is valid on dates 0 to counts[t] - 1; some tile is valid on all 32 dates. scenes are finite reflectances.
All inputs are finite; a program needn't handle non-finite values.
Results may differ from a plain program's by a relative error of at most 0.0005.
Values may be sent and summed in bfloat16 or wider, within the bound.
No kernel may reach another device: no remote copies, remote signals or barrier semaphores. Data moves between devices by JAX's collectives and lax.ppermute only.
A program may use at most 64 MiB of HBM per device.

v0:
```python
import jax
import jax.numpy as jnp
from jax import lax
from jax.sharding import PartitionSpec as P


def solve_fit(weight_sum, sum_x, sum_xx, sum_y, sum_xy):
    total = weight_sum[:, None]
    mean_x = sum_x / total
    mean_y = sum_y / total
    spread = sum_xx / total - mean_x * mean_x + 1e-05
    gain = (sum_xy / total - mean_x * mean_y) / spread
    return (gain, mean_y - gain * mean_x)


def fit_sums_of(weight, values, composite, pif_mask):
    fit = weight * pif_mask[None]
    fitted = fit[:, :, None, :] * values
    weight_sum = jnp.sum(fit, axis=(1, 2))
    sum_x = jnp.sum(fitted, axis=(1, 3))
    sum_xx = jnp.sum(fitted * values, axis=(1, 3))
    sum_y = jnp.sum(fit[:, :, None, :] * composite[None], axis=(1, 3))
    sum_xy = jnp.sum(fitted * composite[None], axis=(1, 3))
    return (weight_sum, sum_x, sum_xx, sum_y, sum_xy)


def local(scenes, quality, pif_mask, counts):
    tile_scenes, tile_quality = (
        lax.all_to_all(scenes, "dates", split_axis=1, concat_axis=0, tiled=True),
        lax.all_to_all(quality, "dates", split_axis=1, concat_axis=0, tiled=True),
    )
    date_ids = jnp.arange(tile_scenes.shape[0], dtype=jnp.int32)
    covered = (date_ids[:, None] < counts[None, :]).astype(jnp.float32)
    weight = tile_quality.astype(jnp.float32) * covered[:, :, None]
    values = tile_scenes.astype(jnp.float32)
    weighted = jnp.sum(weight[:, :, None, :] * values, axis=0)
    totals = jnp.sum(weight, axis=0)
    composite = weighted / totals[:, None, :]
    weight_sum, sum_x, sum_xx, sum_y, sum_xy = fit_sums_of(weight, values, composite, pif_mask)
    sums = (
        lax.psum_scatter(weight_sum, "dates", scatter_dimension=0, tiled=True),
        lax.psum_scatter(sum_x, "dates", scatter_dimension=0, tiled=True),
        lax.psum_scatter(sum_xx, "dates", scatter_dimension=0, tiled=True),
        lax.psum_scatter(sum_y, "dates", scatter_dimension=0, tiled=True),
        lax.psum_scatter(sum_xy, "dates", scatter_dimension=0, tiled=True),
    )
    gain, offset = solve_fit(*sums)
    own_values = scenes.astype(jnp.float32)
    return (gain[:, None, :, None] * own_values + offset[:, None, :, None]).astype(jnp.bfloat16)


def solution(mesh):
    placed = (
        P(("groups", "dates"), None, None, None),
        P(("groups", "dates"), None, None),
        P(("groups", "dates"), None),
        P(("groups", "dates")),
    )
    return jax.shard_map(
        local,
        mesh=mesh,
        in_specs=placed,
        out_specs=P(("groups", "dates"), None, None, None),
        check_vma=False,
    )
```

profile of v0, /device:TPU:0, one launch (start us, length us, event | category | flops | bytes accessed | tf_op | source)
XLA Modules:
  0.0 87.5 jit_solution(16721891539199822126)
XLA Ops:
  0.0 1.3 %copy.29 = bf16[2,16,256]{2,0,1:T(2,128)(2,1)} copy(bf16[2,16,256]{2,1,0:T(8,128)(2,1)} %param.5) | data formatting | bytes 32768 | tf_op args[1]
  1.3 7.4 %all-to-all-start = ((bf16[2,16,256]{2,0,1:T(2,128)(2,1)}), bf16[2,16,256]{2,0,1:T(2,128)(2,1)S(1)}, u32[]{:S(2)}, u32[]{:S(2)}) async-start(bf16[2,16,256]{2,0,1:T(2,128)(2,1)} %copy.29), calls=%async_computation | async-start | bytes 32768 | tf_op jit(solution)/shard_map/all_to_all | solution.py:30
  9.4 1.6 %copy.31 = bf16[2,16,7,256]{3,2,0,1:T(8,128)(2,1)} copy(bf16[2,16,7,256]{3,1,2,0:T(8,128)(2,1)} %param.4) | data formatting | bytes 229376 | tf_op args[0]
  11.0 0.0 copy-start.2
  11.0 0.7 copy-done.2
  11.6 0.6 dynamic-slice
  12.8 2.4 %all-to-all-done = bf16[2,16,256]{2,0,1:T(2,128)(2,1)S(1)} async-done(((bf16[2,16,256]{2,0,1:T(2,128)(2,1)}), bf16[2,16,256]{2,0,1:T(2,128)(2,1)S(1)}, u32[]{:S(2)}, u32[]{:S(2)}) %all-to-all-start) | async-done | bytes 16416 | tf_op jit(solution)/shard_map/all_to_all | solution.py:30
  15.2 3.6 %all-to-all-start.1 = ((bf16[2,16,7,256]{3,2,0,1:T(8,128)(2,1)}), bf16[2,16,7,256]{3,2,0,1:T(8,128)(2,1)S(1)}, u32[]{:S(2)}, u32[]{:S(2)}) async-start(bf16[2,16,7,256]{3,2,0,1:T(8,128)(2,1)} %copy.31), calls=%async_computation.1 | async-start | bytes 262144 | tf_op jit(solution)/shard_map/all_to_all | solution.py:29
  18.9 0.1 reshape.216
  18.9 0.0 copy-start.1
  19.0 0.7 copy-done.1
  19.6 0.1 fusion.7
  19.7 0.5 multiply_reduce_fusion.1
  20.2 0.1 multiply_multiply_fusion.2
  20.3 6.4 %all-to-all-done.1 = bf16[2,16,7,256]{3,2,0,1:T(8,128)(2,1)S(1)} async-done(((bf16[2,16,7,256]{3,2,0,1:T(8,128)(2,1)}), bf16[2,16,7,256]{3,2,0,1:T(8,128)(2,1)S(1)}, u32[]{:S(2)}, u32[]{:S(2)}) %all-to-all-start.1) | async-done | bytes 114720 | tf_op jit(solution)/shard_map/all_to_all | solution.py:29
  26.8 0.1 fusion.6
  26.8 0.2 fusion.2
  27.0 0.0 copy-start
  27.1 0.1 copy.35
  27.1 0.1 copy.40
  27.2 0.1 multiply_reduce_fusion
  27.4 0.1 copy.38
  27.4 0.1 copy.37
  27.5 59.0 %all-reduce.5 = (f32[32,7]{1,0:T(8,128)S(1)}, f32[32,7]{1,0:T(8,128)S(1)}, f32[32]{0:T(128)S(1)}, f32[32,7]{1,0:T(8,128)S(1)}, f32[32,7]{1,0:T(8,128)S(1)}) all-reduce(f32[32,7]{1,0:T(8,128)S(1)} %bitcast.57, f32[32,7]{1,0:T(8,128)S(1)} %bitcast.58, ...), channel_id=2, replica_groups=mesh['groups'=2,'dates'=16] {'dates'}, use_global_device_ids=true, to_apply=%region_3.0.clone | all-reduce | flops 928 | bytes 7424
  86.6 0.1 dynamic-slice.3
  86.6 0.1 multiply_subtract_fusion
  86.7 0.0 copy-done
  86.7 0.8 add_convert_fusion
  (7 shorter events, 0.1 us)
Async XLA Ops:
  1.3 13.9 %all-to-all-start = ((bf16[2,16,256]{2,0,1:T(2,128)(2,1)}), bf16[2,16,256]{2,0,1:T(2,128)(2,1)S(1)}, u32[]{:S(2)}, u32[]{:S(2)}) async-start(bf16[2,16,256]{2,0,1:T(2,128)(2,1)} %copy.29), calls=%async_computation | async-start | bytes 32768 | tf_op jit(solution)/shard_map/all_to_all | solution.py:30
  11.0 0.7 copy-start.2
  15.2 11.5 %all-to-all-start.1 = ((bf16[2,16,7,256]{3,2,0,1:T(8,128)(2,1)}), bf16[2,16,7,256]{3,2,0,1:T(8,128)(2,1)S(1)}, u32[]{:S(2)}, u32[]{:S(2)}) async-start(bf16[2,16,7,256]{3,2,0,1:T(8,128)(2,1)} %copy.31), calls=%async_computation.1 | async-start | bytes 262144 | tf_op jit(solution)/shard_map/all_to_all | solution.py:29
  18.9 0.7 copy-start.1
  27.0 59.7 %copy-start = (bf16[2,16,7,256]{3,1,2,0:T(8,128)(2,1)S(1)}, bf16[2,16,7,256]{3,1,2,0:T(8,128)(2,1)}, u32[]{:S(2)}) copy-start(bf16[2,16,7,256]{3,1,2,0:T(8,128)(2,1)} %param.4) | copy-start | bytes 344068
where the time goes:
time: 87.9 us; the launch traced here: 87.5 us
  blocking collectives  59 us (67%)
  starting transfers between devices  11 us (13%)
  waiting for transfers between devices  8.88 us (10%)
  local copies, waits for them, and re-layouts  5.36 us (6%)
  other arithmetic  1.88 us (2%)
  between operations  1.35 us (2%)
    unnamed x1, blocking collectives  59 us
    all_to_all x1, starting transfers between devices, local(): lax.all_to_all(quality, 'dates', split_axis=1, concat_axis=0, tiled=True)  7.39 us
    all_to_all x1, waiting for transfers between devices, local(): lax.all_to_all(scenes, 'dates', split_axis=1, concat_axis=0, tiled=True)  6.45 us
    unnamed x10, local copies, waits for them, and re-layouts  4.9 us
    all_to_all x1, starting transfers between devices, local(): lax.all_to_all(scenes, 'dates', split_axis=1, concat_axis=0, tiled=True)  3.6 us
    all_to_all x1, waiting for transfers between devices, local(): lax.all_to_all(quality, 'dates', split_axis=1, concat_axis=0, tiled=True)  2.44 us
  transfers between devices with their start and end apart: 2, of which 2 were waited for; matrix products, arithmetic and copies ran while one was open for 3% of the time, Pallas kernels for 0%

commit v1 on v0

v1 whole, which is shorter than its diff:
```python
import functools
import jax
import jax.numpy as jnp
from jax import lax
from jax.experimental import pallas as pl
from jax.experimental.pallas import tpu as pltpu
from jax.sharding import PartitionSpec as P

F32 = jnp.float32
LANES = 128
VMEM = pl.BlockSpec(memory_space=pltpu.VMEM)
SMEM = pl.BlockSpec(memory_space=pltpu.SMEM)


def near(x):
    return pltpu.with_memory_space_constraint(x, pltpu.VMEM)


def tile_kernel(size, pif_ref, counts_ref, out_ref):
    half, width = out_ref.shape
    pixels = pif_ref.shape[-1]
    me = lax.axis_index("dates")
    row = lax.broadcasted_iota(jnp.int32, (half, width), 0)
    count = jnp.full((half, LANES), counts_ref[0], jnp.int32).astype(F32)
    pif = jnp.broadcast_to(pif_ref[...], (half, pixels))
    tile = jnp.concatenate([pif, count], axis=1)
    out_ref[...] = jnp.where(row == me % (size // 2), tile, 0.0)


def split_kernel(size, scenes_ref, quality_ref, keep_ref, send_ref, copy_ref):
    dates, bands, tiles, _ = scenes_ref.shape
    half = tiles // 2
    low = lax.axis_index("dates") < size // 2
    for d in range(dates):
        for b in range(bands + 1):
            whole = scenes_ref[d, b] if b < bands else quality_ref[d]
            if b < bands:
                copy_ref[d, b] = whole
            whole = whole.astype(F32)
            lower, upper = whole[:half], whole[half:]
            keep_ref[d, b] = jnp.where(low, lower, upper).astype(keep_ref.dtype)
            send_ref[d, b] = jnp.where(low, upper, lower).astype(send_ref.dtype)


def weight_of(quality, date, count):
    covered = (count > date.astype(F32)).astype(F32)
    return quality.astype(F32) * jnp.concatenate(
        [covered] * (quality.shape[-1] // LANES), axis=1
    )


def first_dates(size, dates):
    me = lax.axis_index("dates")
    return me * dates, (me ^ (size // 2)) * dates


def partial_kernel(size, keep_ref, got_ref, tile_ref, out_ref):
    dates, rows, half, pixels = keep_ref.shape
    count = tile_ref[:, pixels:]
    weights = [
        (ref, d, weight_of(ref[d, rows - 1], first + d, count))
        for first, ref in zip(first_dates(size, dates), (keep_ref, got_ref))
        for d in range(dates)
    ]
    for b in range(rows - 1):
        out_ref[b] = sum(w * ref[d, b].astype(F32) for ref, d, w in weights)
    out_ref[rows - 1] = sum(w for _, _, w in weights)


def fold(term):
    pixels = term.shape[-1]
    term = sum(term[:, p : p + LANES] for p in range(0, pixels, LANES))
    return jnp.sum(term, axis=0, keepdims=True)


def fit_kernel(size, keep_ref, got_ref, tile_ref, *refs):
    *part_refs, own_ref, other_ref = refs
    dates, rows, half, pixels = keep_ref.shape
    count, pif = tile_ref[:, pixels:], tile_ref[:, :pixels]
    total = [sum(ref[b] for ref in part_refs) for b in range(rows)]
    composite = [total[b] / total[rows - 1] for b in range(rows - 1)]
    sides = zip(first_dates(size, dates), (keep_ref, got_ref), (own_ref, other_ref))
    for first, ref, out in sides:
        for d in range(dates):
            fit = weight_of(ref[d, rows - 1], first + d, count) * pif
            sums = ([], [], [], [])
            for b in range(rows - 1):
                x, y = ref[d, b].astype(F32), composite[b]
                fitted = fit * x
                for kind, term in zip(sums, (fitted, fitted * x, fit * y, fitted * y)):
                    kind.append(fold(term))
            weight = fold(fit)
            for k, kind in enumerate(sums):
                out[d, k] = jnp.concatenate(kind + [weight], axis=0)


def apply_kernel(own_ref, got_ref, scenes_ref, out_ref):
    dates, bands, tiles, pixels = scenes_ref.shape
    sums = own_ref[...] + got_ref[...]
    sums = jnp.sum(sums, axis=-1, keepdims=True)
    for d in range(dates):
        sum_x, sum_xx, sum_y, sum_xy = (sums[d, k, :bands] for k in range(4))
        total = sums[d, 0, bands : bands + 1]
        mean_x = sum_x / total
        mean_y = sum_y / total
        spread = sum_xx / total - mean_x * mean_x + 1e-05
        gain = (sum_xy / total - mean_x * mean_y) / spread
        offset = mean_y - gain * mean_x
        for b in range(bands):
            values = scenes_ref[d, b].astype(F32)
            out_ref[d, b] = (gain[b : b + 1] * values + offset[b : b + 1]).astype(
                out_ref.dtype
            )


def local(size, scenes, quality, pif_mask, counts):
    dates, tiles, bands, pixels = scenes.shape
    scenes = scenes.transpose(0, 2, 1, 3)
    rows, half = bands + 1, tiles // 2
    top = size // 2

    def swap(x, k):
        return lax.ppermute(x, "dates", [(i, i ^ k) for i in range(size)])

    def add_up(x, keep_last=False):
        bit, groups = 1, []
        while bit < top:
            wide = bit > 1 and bit * 2 < top
            groups.append([3 * bit, 2 * bit, bit] if wide else [bit])
            bit *= 4 if wide else 2
        for group in groups[: -1 if keep_last else None]:
            x = sum([swap(x, k) for k in group[::-1]], x)
        if keep_last:
            return [x] + [swap(x, k) for k in groups[-1][::-1]]
        return x

    tile = pl.pallas_call(
        functools.partial(tile_kernel, size),
        out_shape=pltpu.VMEM((half, pixels + LANES), F32),
        in_specs=[VMEM, SMEM],
        out_specs=VMEM,
    )(pif_mask, counts)
    tile = near(add_up(tile))
    shape = (dates, rows, half, pixels)
    keep, send, copy = pl.pallas_call(
        functools.partial(split_kernel, size),
        out_shape=[
            pltpu.VMEM(shape, scenes.dtype),
            pltpu.VMEM(shape, scenes.dtype),
            pltpu.VMEM(scenes.shape, scenes.dtype),
        ],
        in_specs=[VMEM, VMEM],
        out_specs=[VMEM] * 3,
    )(scenes, quality)
    got = near(swap(send, top))
    keep, copy = near(keep), near(copy)
    part = pl.pallas_call(
        functools.partial(partial_kernel, size),
        out_shape=pltpu.VMEM(shape[1:], F32),
        in_specs=[VMEM] * 3,
        out_specs=VMEM,
    )(keep, got, tile)
    parts = add_up(part, keep_last=True)
    sums = pltpu.VMEM((dates, 4, rows, LANES), F32)
    own, other = pl.pallas_call(
        functools.partial(fit_kernel, size),
        out_shape=[sums, sums],
        in_specs=[VMEM] * (3 + len(parts)),
        out_specs=[VMEM] * 2,
    )(keep, got, tile, *map(near, parts))
    out = pl.pallas_call(
        apply_kernel,
        out_shape=jax.ShapeDtypeStruct(scenes.shape, scenes.dtype),
        in_specs=[VMEM] * 3,
        out_specs=VMEM,
    )(near(own), near(swap(other, top)), copy)
    return out.transpose(0, 2, 1, 3)


def solution(mesh):
    placed = (
        P(("groups", "dates"), None, None, None),
        P(("groups", "dates"), None, None),
        P(("groups", "dates"), None),
        P(("groups", "dates")),
    )
    return jax.shard_map(
        functools.partial(local, mesh.shape["dates"]),
        mesh=mesh,
        in_specs=placed,
        out_specs=P(("groups", "dates"), None, None, None),
        check_vma=False,
    )
```

time: 87.9 us -> 28.4 us (0.32)
  blocking collectives: 59 us -> 0 us
  local copies, waits for them, and re-layouts: 5.36 us -> 0 us
  starting transfers between devices: 11 us -> 14.3 us
  Pallas kernels: 0 us -> 2.62 us
  other arithmetic: 1.88 us -> 0.02 us
  waiting for transfers between devices: 8.88 us -> 10.6 us
    unnamed x1 -> x0, blocking collectives: 59 us -> none
    ppermute x0 -> x10, starting transfers between devices: none -> 14.3 us  [swap(): return lax.ppermute(x, 'dates', [(i, i ^ k) for i in range(size)])]
    all_to_all x2 -> x0, starting transfers between devices: 11 us -> none  [the longest x1 7.39 us: local(): lax.all_to_all(quality, 'dates', split_axis=1, concat_axis=0, tiled=True)]
    ppermute x0 -> x10, waiting for transfers between devices: none -> 10.6 us  [swap(): return lax.ppermute(x, 'dates', [(i, i ^ k) for i in range(size)])]
    all_to_all x2 -> x0, waiting for transfers between devices: 8.88 us -> none  [the longest x1 6.45 us: local(): lax.all_to_all(scenes, 'dates', split_axis=1, concat_axis=0, tiled=True)]
    unnamed x10 -> x0, local copies, waits for them, and re-layouts: 4.9 us -> none
    pallas_call x0 -> x5, Pallas kernels: none -> 2.62 us  [the longest x1 0.93 us: local(): pl.pallas_call(functools.partial(split_kernel, size), out_shape=[pltpu.VM...]
  transfers between devices with their start and end apart: 2 -> 10, of which waited for: 2 -> 7; matrix products, arithmetic and copies ran while one was open for 3% -> 0% of each run, Pallas kernels for 0% -> 3%
where the time goes in v1:
time: 28.4 us; the launch traced here: 28.2 us
  starting transfers between devices  14.3 us (50%)
  waiting for transfers between devices  10.6 us (37%)
  Pallas kernels  2.62 us (9%)
  between operations  0.7 us (2%)
    ppermute x10, starting transfers between devices, swap(): return lax.ppermute(x, 'dates', [(i, i ^ k) for i in range(size)])  14.3 us
    ppermute x10, waiting for transfers between devices, swap(): return lax.ppermute(x, 'dates', [(i, i ^ k) for i in range(size)])  10.6 us
    pallas_call x1, Pallas kernels, local(): pl.pallas_call(functools.partial(split_kernel, size), out_shape=[pltpu.VM...  0.93 us
    pallas_call x1, Pallas kernels, local(): pl.pallas_call(apply_kernel, out_shape=jax.ShapeDtypeStruct(scenes.shape,...  0.77 us
    pallas_call x1, Pallas kernels, local(): pl.pallas_call(functools.partial(tile_kernel, size), out_shape=pltpu.VMEM...  0.68 us
  transfers between devices with their start and end apart: 10, of which 7 were waited for; matrix products, arithmetic and copies ran while one was open for 0% of the time, Pallas kernels for 3%

profile of v1, /device:TPU:0, one launch (start us, length us, event | category | flops | bytes accessed | tf_op | source)
XLA Modules:
  0.0 28.2 jit_solution(18072329669524646436)
XLA Ops:
  0.7 0.7 %shard_map.47 = f32[8,384]{1,0:T(8,128)S(1)} custom-call(f32[1,256]{1,0:T(1,128)} %pif_ref.1, s32[1]{0:T(128)S(6)} %copy.5.counts_ref), custom_call_target="tpu_custom_call" | custom-call | tf_op jit(solution)/shard_map/pallas_call | solution.py:137
  1.3 0.5 %collective-permute-start.1 = (f32[8,384]{1,0:T(8,128)S(1)}, f32[8,384]{1,0:T(8,128)S(1)}, u32[]{:S(2)}, u32[]{:S(2)}) collective-permute-start(f32[8,384]{1,0:T(8,128)S(1)} %shard_map.47), channel_id=1, source_target_pairs={{0,1},{1,0},{2,3},{3,2},{4,5},{5,4},{6,7},{7,6},{8,9},{9,8},{10,11... | collective-permute-start | bytes 36872 | tf_op jit(solution)/shard_map/ppermute | solution.py:123
  1.8 0.8 %collective-permute-done.1 = f32[8,384]{1,0:T(8,128)S(1)} collective-permute-done((f32[8,384]{1,0:T(8,128)S(1)}, f32[8,384]{1,0:T(8,128)S(1)}, u32[]{:S(2)}, u32[]{:S(2)}) %collective-permute-start.1) | collective-permute-done | bytes 12320 | tf_op jit(solution)/shard_map/ppermute | solution.py:123
  2.6 3.9 %collective-permute-start.4 = (f32[8,384]{1,0:T(8,128)S(1)}, f32[8,384]{1,0:T(8,128)S(1)}, u32[]{:S(2)}, u32[]{:S(2)}) collective-permute-start(f32[8,384]{1,0:T(8,128)S(1)} %add.15), channel_id=1, source_target_pairs={{0,6},{1,7},{2,4},{3,5},{4,2},{5,3},{6,0},{7,1},{8,14},{9,15},{10,... | collective-permute-start | bytes 36872 | tf_op jit(solution)/shard_map/ppermute | solution.py:123
  6.5 0.4 %collective-permute-start.3 = (f32[8,384]{1,0:T(8,128)S(1)}, f32[8,384]{1,0:T(8,128)S(1)}, u32[]{:S(2)}, u32[]{:S(2)}) collective-permute-start(f32[8,384]{1,0:T(8,128)S(1)} %add.15), channel_id=1, source_target_pairs={{0,4},{1,5},{2,6},{3,7},{4,0},{5,1},{6,2},{7,3},{8,12},{9,13},{10,... | collective-permute-start | bytes 36872 | tf_op jit(solution)/shard_map/ppermute | solution.py:123
  6.9 0.1 collective-permute-start.2
  7.1 0.9 %shard_map.46 = (bf16[2,8,8,256]{3,2,1,0:T(8,128)(2,1)S(1)}, bf16[2,8,8,256]{3,2,1,0:T(8,128)(2,1)S(1)}, bf16[2,7,16,256]{3,2,1,0:T(8,128)(2,1)S(1)}) custom-call(bf16[2,7,16,256]{3,2,1,0:T(8,128)(2,1)} %bitcast.2, bf16[2,16,256]{2,1,0:T(8,128)(2,1)} %quality_ref.1), custom_call_target="tpu_custom_call" | custom-call | tf_op jit(solution)/shard_map/pallas_call | solution.py:145
  8.0 3.0 %collective-permute-start = (bf16[2,8,8,256]{3,2,1,0:T(8,128)(2,1)S(1)}, bf16[2,8,8,256]{3,2,1,0:T(8,128)(2,1)S(1)}, u32[]{:S(2)}, u32[]{:S(2)}) collective-permute-start(bf16[2,8,8,256]{3,2,1,0:T(8,128)(2,1)S(1)} %get-tuple-element.11), channel_id=1, source_target_pairs={{0,8},{1,9},{2,10},{3,11},{4,12},{5,13},{6,14},{7,15},{8,0},{9,1},... | collective-permute-start | bytes 196616 | tf_op jit(solution)/shard_map/ppermute | solution.py:123
  11.0 0.0 collective-permute-done.4
  11.1 0.0 collective-permute-done.3
  11.1 0.0 collective-permute-done.2
  11.1 2.6 %collective-permute-done.got_ref = bf16[2,8,8,256]{3,2,1,0:T(8,128)(2,1)S(1)} collective-permute-done((bf16[2,8,8,256]{3,2,1,0:T(8,128)(2,1)S(1)}, bf16[2,8,8,256]{3,2,1,0:T(8,128)(2,1)S(1)}, u32[]{:S(2)}, u32[]{:S(2)}) %collective-permute-start) | collective-permute-done | bytes 65568 | tf_op jit(solution)/shard_map/ppermute | solution.py:123
  13.7 0.1 collective-permute-start.5
  13.8 1.2 %collective-permute-done.5 = f32[8,8,256]{2,1,0:T(8,128)S(1)} collective-permute-done((f32[8,8,256]{2,1,0:T(8,128)S(1)}, f32[8,8,256]{2,1,0:T(8,128)S(1)}, u32[]{:S(2)}, u32[]{:S(2)}) %collective-permute-start.5) | collective-permute-done | bytes 65568 | tf_op jit(solution)/shard_map/ppermute | solution.py:123
  15.1 2.5 %collective-permute-start.8 = (f32[8,8,256]{2,1,0:T(8,128)S(1)}, f32[8,8,256]{2,1,0:T(8,128)S(1)}, u32[]{:S(2)}, u32[]{:S(2)}) collective-permute-start(f32[8,8,256]{2,1,0:T(8,128)S(1)} %add.19.refs_0_), channel_id=1, source_target_pairs={{0,6},{1,7},{2,4},{3,5},{4,2},{5,3},{6,0},{7,1},{8,14},{9,15},{10,... | collective-permute-start | bytes 196616 | tf_op jit(solution)/shard_map/ppermute | solution.py:123
  17.6 0.5 %collective-permute-start.7 = (f32[8,8,256]{2,1,0:T(8,128)S(1)}, f32[8,8,256]{2,1,0:T(8,128)S(1)}, u32[]{:S(2)}, u32[]{:S(2)}) collective-permute-start(f32[8,8,256]{2,1,0:T(8,128)S(1)} %add.19.refs_0_), channel_id=1, source_target_pairs={{0,4},{1,5},{2,6},{3,7},{4,0},{5,1},{6,2},{7,3},{8,12},{9,13},{10,... | collective-permute-start | bytes 196616 | tf_op jit(solution)/shard_map/ppermute | solution.py:123
  18.1 0.5 %collective-permute-start.6 = (f32[8,8,256]{2,1,0:T(8,128)S(1)}, f32[8,8,256]{2,1,0:T(8,128)S(1)}, u32[]{:S(2)}, u32[]{:S(2)}) collective-permute-start(f32[8,8,256]{2,1,0:T(8,128)S(1)} %add.19.refs_0_), channel_id=1, source_target_pairs={{0,2},{1,3},{2,0},{3,1},{4,6},{5,7},{6,4},{7,5},{8,10},{9,11},{10,... | collective-permute-start | bytes 196616 | tf_op jit(solution)/shard_map/ppermute | solution.py:123
  18.6 2.0 %collective-permute-done.8.refs_3_ = f32[8,8,256]{2,1,0:T(8,128)S(1)} collective-permute-done((f32[8,8,256]{2,1,0:T(8,128)S(1)}, f32[8,8,256]{2,1,0:T(8,128)S(1)}, u32[]{:S(2)}, u32[]{:S(2)}) %collective-permute-start.8) | collective-permute-done | bytes 65568 | tf_op jit(solution)/shard_map/ppermute | solution.py:123
  20.7 1.2 %collective-permute-done.7.refs_2_ = f32[8,8,256]{2,1,0:T(8,128)S(1)} collective-permute-done((f32[8,8,256]{2,1,0:T(8,128)S(1)}, f32[8,8,256]{2,1,0:T(8,128)S(1)}, u32[]{:S(2)}, u32[]{:S(2)}) %collective-permute-start.7) | collective-permute-done | bytes 65568 | tf_op jit(solution)/shard_map/ppermute | solution.py:123
  21.9 0.5 %collective-permute-done.6.refs_1_ = f32[8,8,256]{2,1,0:T(8,128)S(1)} collective-permute-done((f32[8,8,256]{2,1,0:T(8,128)S(1)}, f32[8,8,256]{2,1,0:T(8,128)S(1)}, u32[]{:S(2)}, u32[]{:S(2)}) %collective-permute-start.6) | collective-permute-done | bytes 65568 | tf_op jit(solution)/shard_map/ppermute | solution.py:123
  22.4 0.2 shard_map.49
  22.6 2.7 %collective-permute-start.9 = (f32[2,4,8,128]{3,2,1,0:T(8,128)S(1)}, f32[2,4,8,128]{3,2,1,0:T(8,128)S(1)}, u32[]{:S(2)}, u32[]{:S(2)}) collective-permute-start(f32[2,4,8,128]{3,2,1,0:T(8,128)S(1)} %get-tuple-element.13), channel_id=1, source_target_pairs={{0,8},{1,9},{2,10},{3,11},{4,12},{5,13},{6,14},{7,15},{8,0},{9,1},... | collective-permute-start | bytes 98312 | tf_op jit(solution)/shard_map/ppermute | solution.py:123
  25.3 2.2 %collective-permute-done.9.got_ref = f32[2,4,8,128]{3,2,1,0:T(8,128)S(1)} collective-permute-done((f32[2,4,8,128]{3,2,1,0:T(8,128)S(1)}, f32[2,4,8,128]{3,2,1,0:T(8,128)S(1)}, u32[]{:S(2)}, u32[]{:S(2)}) %collective-permute-start.9) | collective-permute-done | bytes 32800 | tf_op jit(solution)/shard_map/ppermute | solution.py:123
  27.5 0.8 %shard_map.50 = bf16[2,7,16,256]{3,2,1,0:T(8,128)(2,1)} custom-call(f32[2,4,8,128]{3,2,1,0:T(8,128)S(1)} %get-tuple-element.12.own_ref, f32[2,4,8,128]{3,2,1,0:T(8,128)S(1)} %collective-permute-done.9.got_ref, bf16[2,7,16,256]{3,2,1,0:T(8,128)(2,1)S(1)} %get-tuple-element.14.scenes_ref), custom_call_target="tpu_custom_call" | custom-call | tf_op jit(solution)/shard_map/pallas_call | solution.py:171
  (4 shorter events, 0.1 us)
Async XLA Ops:
  1.3 1.3 %collective-permute-start.1 = (f32[8,384]{1,0:T(8,128)S(1)}, f32[8,384]{1,0:T(8,128)S(1)}, u32[]{:S(2)}, u32[]{:S(2)}) collective-permute-start(f32[8,384]{1,0:T(8,128)S(1)} %shard_map.47), channel_id=1, source_target_pairs={{0,1},{1,0},{2,3},{3,2},{4,5},{5,4},{6,7},{7,6},{8,9},{9,8},{10,11... | collective-permute-start | bytes 36872 | tf_op jit(solution)/shard_map/ppermute | solution.py:123
  2.6 8.4 %collective-permute-start.4 = (f32[8,384]{1,0:T(8,128)S(1)}, f32[8,384]{1,0:T(8,128)S(1)}, u32[]{:S(2)}, u32[]{:S(2)}) collective-permute-start(f32[8,384]{1,0:T(8,128)S(1)} %add.15), channel_id=1, source_target_pairs={{0,6},{1,7},{2,4},{3,5},{4,2},{5,3},{6,0},{7,1},{8,14},{9,15},{10,... | collective-permute-start | bytes 36872 | tf_op jit(solution)/shard_map/ppermute | solution.py:123
  6.5 4.6 %collective-permute-start.3 = (f32[8,384]{1,0:T(8,128)S(1)}, f32[8,384]{1,0:T(8,128)S(1)}, u32[]{:S(2)}, u32[]{:S(2)}) collective-permute-start(f32[8,384]{1,0:T(8,128)S(1)} %add.15), channel_id=1, source_target_pairs={{0,4},{1,5},{2,6},{3,7},{4,0},{5,1},{6,2},{7,3},{8,12},{9,13},{10,... | collective-permute-start | bytes 36872 | tf_op jit(solution)/shard_map/ppermute | solution.py:123
  6.9 4.1 %collective-permute-start.2 = (f32[8,384]{1,0:T(8,128)S(1)}, f32[8,384]{1,0:T(8,128)S(1)}, u32[]{:S(2)}, u32[]{:S(2)}) collective-permute-start(f32[8,384]{1,0:T(8,128)S(1)} %add.15), channel_id=1, source_target_pairs={{0,2},{1,3},{2,0},{3,1},{4,6},{5,7},{6,4},{7,5},{8,10},{9,11},{10,... | collective-permute-start | bytes 36872 | tf_op jit(solution)/shard_map/ppermute | solution.py:123
  8.0 5.7 %collective-permute-start = (bf16[2,8,8,256]{3,2,1,0:T(8,128)(2,1)S(1)}, bf16[2,8,8,256]{3,2,1,0:T(8,128)(2,1)S(1)}, u32[]{:S(2)}, u32[]{:S(2)}) collective-permute-start(bf16[2,8,8,256]{3,2,1,0:T(8,128)(2,1)S(1)} %get-tuple-element.11), channel_id=1, source_target_pairs={{0,8},{1,9},{2,10},{3,11},{4,12},{5,13},{6,14},{7,15},{8,0},{9,1},... | collective-permute-start | bytes 196616 | tf_op jit(solution)/shard_map/ppermute | solution.py:123
  13.7 1.3 %collective-permute-start.5 = (f32[8,8,256]{2,1,0:T(8,128)S(1)}, f32[8,8,256]{2,1,0:T(8,128)S(1)}, u32[]{:S(2)}, u32[]{:S(2)}) collective-permute-start(f32[8,8,256]{2,1,0:T(8,128)S(1)} %shard_map.48), channel_id=1, source_target_pairs={{0,1},{1,0},{2,3},{3,2},{4,5},{5,4},{6,7},{7,6},{8,9},{9,8},{10,11... | collective-permute-start | bytes 196616 | tf_op jit(solution)/shard_map/ppermute | solution.py:123
  15.1 5.6 %collective-permute-start.8 = (f32[8,8,256]{2,1,0:T(8,128)S(1)}, f32[8,8,256]{2,1,0:T(8,128)S(1)}, u32[]{:S(2)}, u32[]{:S(2)}) collective-permute-start(f32[8,8,256]{2,1,0:T(8,128)S(1)} %add.19.refs_0_), channel_id=1, source_target_pairs={{0,6},{1,7},{2,4},{3,5},{4,2},{5,3},{6,0},{7,1},{8,14},{9,15},{10,... | collective-permute-start | bytes 196616 | tf_op jit(solution)/shard_map/ppermute | solution.py:123
  17.6 4.3 %collective-permute-start.7 = (f32[8,8,256]{2,1,0:T(8,128)S(1)}, f32[8,8,256]{2,1,0:T(8,128)S(1)}, u32[]{:S(2)}, u32[]{:S(2)}) collective-permute-start(f32[8,8,256]{2,1,0:T(8,128)S(1)} %add.19.refs_0_), channel_id=1, source_target_pairs={{0,4},{1,5},{2,6},{3,7},{4,0},{5,1},{6,2},{7,3},{8,12},{9,13},{10,... | collective-permute-start | bytes 196616 | tf_op jit(solution)/shard_map/ppermute | solution.py:123
  18.1 4.3 %collective-permute-start.6 = (f32[8,8,256]{2,1,0:T(8,128)S(1)}, f32[8,8,256]{2,1,0:T(8,128)S(1)}, u32[]{:S(2)}, u32[]{:S(2)}) collective-permute-start(f32[8,8,256]{2,1,0:T(8,128)S(1)} %add.19.refs_0_), channel_id=1, source_target_pairs={{0,2},{1,3},{2,0},{3,1},{4,6},{5,7},{6,4},{7,5},{8,10},{9,11},{10,... | collective-permute-start | bytes 196616 | tf_op jit(solution)/shard_map/ppermute | solution.py:123
  22.6 4.9 %collective-permute-start.9 = (f32[2,4,8,128]{3,2,1,0:T(8,128)S(1)}, f32[2,4,8,128]{3,2,1,0:T(8,128)S(1)}, u32[]{:S(2)}, u32[]{:S(2)}) collective-permute-start(f32[2,4,8,128]{3,2,1,0:T(8,128)S(1)} %get-tuple-element.13), channel_id=1, source_target_pairs={{0,8},{1,9},{2,10},{3,11},{4,12},{5,13},{6,14},{7,15},{8,0},{9,1},... | collective-permute-start | bytes 98312 | tf_op jit(solution)/shard_map/ppermute | solution.py:123

commit v2 on v1

--- a/solution.py
+++ b/solution.py
@@ -16,21 +16,18 @@
     return pltpu.with_memory_space_constraint(x, pltpu.VMEM)
 
 
-def tile_kernel(size, pif_ref, counts_ref, out_ref):
-    half, width = out_ref.shape
-    pixels = pif_ref.shape[-1]
+def split_kernel(
+    size, scenes_ref, quality_ref, pif_ref, counts_ref, tile_ref, keep_ref, send_ref, copy_ref
+):
+    dates, bands, tiles, pixels = scenes_ref.shape
+    half = tiles // 2
     me = lax.axis_index("dates")
-    row = lax.broadcasted_iota(jnp.int32, (half, width), 0)
-    count = jnp.full((half, LANES), counts_ref[0], jnp.int32).astype(F32)
+    row = lax.broadcasted_iota(jnp.int32, tile_ref.shape, 0)
+    count = jnp.broadcast_to(counts_ref[...].astype(F32), (half, LANES))
     pif = jnp.broadcast_to(pif_ref[...], (half, pixels))
     tile = jnp.concatenate([pif, count], axis=1)
-    out_ref[...] = jnp.where(row == me % (size // 2), tile, 0.0)
-
-
-def split_kernel(size, scenes_ref, quality_ref, keep_ref, send_ref, copy_ref):
-    dates, bands, tiles, _ = scenes_ref.shape
-    half = tiles // 2
-    low = lax.axis_index("dates") < size // 2
+    tile_ref[...] = jnp.where(row == me % (size // 2), tile, 0.0)
+    low = me < size // 2
     for d in range(dates):
         for b in range(bands + 1):
             whole = scenes_ref[d, b] if b < bands else quality_ref[d]
@@ -122,36 +119,30 @@
     def swap(x, k):
         return lax.ppermute(x, "dates", [(i, i ^ k) for i in range(size)])
 
-    def add_up(x, keep_last=False):
-        bit, groups = 1, []
-        while bit < top:
-            wide = bit > 1 and bit * 2 < top
-            groups.append([3 * bit, 2 * bit, bit] if wide else [bit])
-            bit *= 4 if wide else 2
-        for group in groups[: -1 if keep_last else None]:
-            x = sum([swap(x, k) for k in group[::-1]], x)
-        if keep_last:
-            return [x] + [swap(x, k) for k in groups[-1][::-1]]
-        return x
+    bit, groups = 2, []
+    while bit < top:
+        wide = bit * 2 < top
+        groups.append([3 * bit, 2 * bit, bit] if wide else [bit])
+        bit *= 4 if wide else 2
 
-    tile = pl.pallas_call(
-        functools.partial(tile_kernel, size),
-        out_shape=pltpu.VMEM((half, pixels + LANES), F32),
-        in_specs=[VMEM, SMEM],
-        out_specs=VMEM,
-    )(pif_mask, counts)
-    tile = near(add_up(tile))
+    def parts_of(x, group):
+        return [x] + [swap(x, k) for k in group[::-1]]
+
     shape = (dates, rows, half, pixels)
-    keep, send, copy = pl.pallas_call(
+    tile, keep, send, copy = pl.pallas_call(
         functools.partial(split_kernel, size),
         out_shape=[
+            pltpu.VMEM((half, pixels + LANES), F32),
             pltpu.VMEM(shape, scenes.dtype),
             pltpu.VMEM(shape, scenes.dtype),
             pltpu.VMEM(scenes.shape, scenes.dtype),
         ],
-        in_specs=[VMEM, VMEM],
-        out_specs=[VMEM] * 3,
-    )(scenes, quality)
+        in_specs=[VMEM] * 4,
+        out_specs=[VMEM] * 4,
+    )(scenes, quality, pif_mask, counts[None])
+    for group in groups:
+        tile = sum(parts_of(tile, group))
+    tile = near(tile + swap(tile, 1))
     got = near(swap(send, top))
     keep, copy = near(keep), near(copy)
     part = pl.pallas_call(
@@ -160,7 +151,9 @@
         in_specs=[VMEM] * 3,
         out_specs=VMEM,
     )(keep, got, tile)
-    parts = add_up(part, keep_last=True)
+    parts = parts_of(part, [1])
+    for group in groups:
+        parts = parts_of(sum(parts), group)
     sums = pltpu.VMEM((dates, 4, rows, LANES), F32)
     own, other = pl.pallas_call(
         functools.partial(fit_kernel, size),

time: 28.4 us -> 26.5 us (0.933)
  waiting for transfers between devices: 10.6 us -> 9.57 us
  Pallas kernels: 2.62 us -> 1.99 us
    ppermute x10, waiting for transfers between devices: 10.6 us -> 9.57 us  [swap(): return lax.ppermute(x, 'dates', [(i, i ^ k) for i in range(size)])]
    pallas_call x1 -> x0, Pallas kernels: 0.68 us -> none  [local(): pl.pallas_call(functools.partial(tile_kernel, size), out_shape=pltpu.VMEM...]
  transfers between devices with their start and end apart: 10 -> 10, of which waited for: 7 -> 8; matrix products, arithmetic and copies ran while one was open for 0% -> 0% of each run, Pallas kernels for 3% -> 0%
where the time goes in v2:
time: 26.5 us; the launch traced here: 26.3 us
  starting transfers between devices  14.1 us (53%)
  waiting for transfers between devices  9.57 us (36%)
  Pallas kernels  1.99 us (8%)
  between operations  0.69 us (3%)
    ppermute x10, starting transfers between devices, swap(): return lax.ppermute(x, 'dates', [(i, i ^ k) for i in range(size)])  14.1 us
    ppermute x10, waiting for transfers between devices, swap(): return lax.ppermute(x, 'dates', [(i, i ^ k) for i in range(size)])  9.57 us
    pallas_call x1, Pallas kernels, local(): pl.pallas_call(functools.partial(split_kernel, size), out_shape=[pltpu.VM...  0.99 us
    pallas_call x1, Pallas kernels, local(): pl.pallas_call(apply_kernel, out_shape=jax.ShapeDtypeStruct(scenes.shape,...  0.77 us
  transfers between devices with their start and end apart: 10, of which 8 were waited for; matrix products, arithmetic and copies ran while one was open for 0% of the time, Pallas kernels for 0%

profile of v2, /device:TPU:0, one launch (start us, length us, event | category | flops | bytes accessed | tf_op | source)
XLA Modules:
  0.0 26.3 jit_solution(653353427046892247)
XLA Ops:
  0.7 1.0 %shard_map.46 = (f32[8,384]{1,0:T(8,128)S(1)}, bf16[2,8,8,256]{3,2,1,0:T(8,128)(2,1)S(1)}, bf16[2,8,8,256]{3,2,1,0:T(8,128)(2,1)S(1)}, bf16[2,7,16,256]{3,2,1,0:T(8,128)(2,1)S(1)}) custom-call(bf16[2,7,16,256]{3,2,1,0:T(8,128)(2,1)} %bitcast.4, bf16[2,16,256]{2,1,0:T(8,128)(2,1)} %quality_ref.1, f32[1,256]{1,0:T(1,128)} %pif_ref.1, s32[1,1]{1,0:T(1,128)} %bitcast.3.counts_ref), custom_call_target="tpu_custom_call" | custom-call | tf_op jit(solution)/shard_map/pallas_call | solution.py:132
  1.6 4.0 %collective-permute-start.3 = (f32[8,384]{1,0:T(8,128)S(1)}, f32[8,384]{1,0:T(8,128)S(1)}, u32[]{:S(2)}, u32[]{:S(2)}) collective-permute-start(f32[8,384]{1,0:T(8,128)S(1)} %get-tuple-element.13), channel_id=1, source_target_pairs={{0,6},{1,7},{2,4},{3,5},{4,2},{5,3},{6,0},{7,1},{8,14},{9,15},{10,... | collective-permute-start | bytes 36872 | tf_op jit(solution)/shard_map/ppermute | solution.py:120
  5.7 0.4 %collective-permute-start.2 = (f32[8,384]{1,0:T(8,128)S(1)}, f32[8,384]{1,0:T(8,128)S(1)}, u32[]{:S(2)}, u32[]{:S(2)}) collective-permute-start(f32[8,384]{1,0:T(8,128)S(1)} %get-tuple-element.13), channel_id=1, source_target_pairs={{0,4},{1,5},{2,6},{3,7},{4,0},{5,1},{6,2},{7,3},{8,12},{9,13},{10,... | collective-permute-start | bytes 36872 | tf_op jit(solution)/shard_map/ppermute | solution.py:120
  6.1 0.2 collective-permute-start.1
  6.3 2.9 %collective-permute-start = (bf16[2,8,8,256]{3,2,1,0:T(8,128)(2,1)S(1)}, bf16[2,8,8,256]{3,2,1,0:T(8,128)(2,1)S(1)}, u32[]{:S(2)}, u32[]{:S(2)}) collective-permute-start(bf16[2,8,8,256]{3,2,1,0:T(8,128)(2,1)S(1)} %get-tuple-element.12), channel_id=1, source_target_pairs={{0,8},{1,9},{2,10},{3,11},{4,12},{5,13},{6,14},{7,15},{8,0},{9,1},... | collective-permute-start | bytes 196616 | tf_op jit(solution)/shard_map/ppermute | solution.py:120
  9.2 0.0 collective-permute-done.3
  9.2 0.7 %collective-permute-done.2 = f32[8,384]{1,0:T(8,128)S(1)} collective-permute-done((f32[8,384]{1,0:T(8,128)S(1)}, f32[8,384]{1,0:T(8,128)S(1)}, u32[]{:S(2)}, u32[]{:S(2)}) %collective-permute-start.2) | collective-permute-done | bytes 12320 | tf_op jit(solution)/shard_map/ppermute | solution.py:120
  9.9 0.0 collective-permute-done.1
  9.9 0.1 collective-permute-start.4
  10.0 1.2 %collective-permute-done.4 = f32[8,384]{1,0:T(8,128)S(1)} collective-permute-done((f32[8,384]{1,0:T(8,128)S(1)}, f32[8,384]{1,0:T(8,128)S(1)}, u32[]{:S(2)}, u32[]{:S(2)}) %collective-permute-start.4) | collective-permute-done | bytes 12320 | tf_op jit(solution)/shard_map/ppermute | solution.py:120
  11.2 0.4 %collective-permute-done.got_ref = bf16[2,8,8,256]{3,2,1,0:T(8,128)(2,1)S(1)} collective-permute-done((bf16[2,8,8,256]{3,2,1,0:T(8,128)(2,1)S(1)}, bf16[2,8,8,256]{3,2,1,0:T(8,128)(2,1)S(1)}, u32[]{:S(2)}, u32[]{:S(2)}) %collective-permute-start) | collective-permute-done | bytes 65568 | tf_op jit(solution)/shard_map/ppermute | solution.py:120
  11.6 0.1 collective-permute-start.5
  11.6 1.2 %collective-permute-done.5 = f32[8,8,256]{2,1,0:T(8,128)S(1)} collective-permute-done((f32[8,8,256]{2,1,0:T(8,128)S(1)}, f32[8,8,256]{2,1,0:T(8,128)S(1)}, u32[]{:S(2)}, u32[]{:S(2)}) %collective-permute-start.5) | collective-permute-done | bytes 65568 | tf_op jit(solution)/shard_map/ppermute | solution.py:120
  12.9 2.9 %collective-permute-start.8 = (f32[8,8,256]{2,1,0:T(8,128)S(1)}, f32[8,8,256]{2,1,0:T(8,128)S(1)}, u32[]{:S(2)}, u32[]{:S(2)}) collective-permute-start(f32[8,8,256]{2,1,0:T(8,128)S(1)} %add.19.refs_0_), channel_id=1, source_target_pairs={{0,6},{1,7},{2,4},{3,5},{4,2},{5,3},{6,0},{7,1},{8,14},{9,15},{10,... | collective-permute-start | bytes 196616 | tf_op jit(solution)/shard_map/ppermute | solution.py:120
  15.8 0.4 %collective-permute-start.7 = (f32[8,8,256]{2,1,0:T(8,128)S(1)}, f32[8,8,256]{2,1,0:T(8,128)S(1)}, u32[]{:S(2)}, u32[]{:S(2)}) collective-permute-start(f32[8,8,256]{2,1,0:T(8,128)S(1)} %add.19.refs_0_), channel_id=1, source_target_pairs={{0,4},{1,5},{2,6},{3,7},{4,0},{5,1},{6,2},{7,3},{8,12},{9,13},{10,... | collective-permute-start | bytes 196616 | tf_op jit(solution)/shard_map/ppermute | solution.py:120
  16.2 0.2 collective-permute-start.6
  16.4 1.7 %collective-permute-done.8.refs_3_ = f32[8,8,256]{2,1,0:T(8,128)S(1)} collective-permute-done((f32[8,8,256]{2,1,0:T(8,128)S(1)}, f32[8,8,256]{2,1,0:T(8,128)S(1)}, u32[]{:S(2)}, u32[]{:S(2)}) %collective-permute-start.8) | collective-permute-done | bytes 65568 | tf_op jit(solution)/shard_map/ppermute | solution.py:120
  18.2 1.9 %collective-permute-done.7.refs_2_ = f32[8,8,256]{2,1,0:T(8,128)S(1)} collective-permute-done((f32[8,8,256]{2,1,0:T(8,128)S(1)}, f32[8,8,256]{2,1,0:T(8,128)S(1)}, u32[]{:S(2)}, u32[]{:S(2)}) %collective-permute-start.7) | collective-permute-done | bytes 65568 | tf_op jit(solution)/shard_map/ppermute | solution.py:120
  20.0 0.4 %collective-permute-done.6.refs_1_ = f32[8,8,256]{2,1,0:T(8,128)S(1)} collective-permute-done((f32[8,8,256]{2,1,0:T(8,128)S(1)}, f32[8,8,256]{2,1,0:T(8,128)S(1)}, u32[]{:S(2)}, u32[]{:S(2)}) %collective-permute-start.6) | collective-permute-done | bytes 65568 | tf_op jit(solution)/shard_map/ppermute | solution.py:120
  20.5 0.2 shard_map.48
  20.7 2.8 %collective-permute-start.9 = (f32[2,4,8,128]{3,2,1,0:T(8,128)S(1)}, f32[2,4,8,128]{3,2,1,0:T(8,128)S(1)}, u32[]{:S(2)}, u32[]{:S(2)}) collective-permute-start(f32[2,4,8,128]{3,2,1,0:T(8,128)S(1)} %get-tuple-element.15), channel_id=1, source_target_pairs={{0,8},{1,9},{2,10},{3,11},{4,12},{5,13},{6,14},{7,15},{8,0},{9,1},... | collective-permute-start | bytes 98312 | tf_op jit(solution)/shard_map/ppermute | solution.py:120
  23.5 2.1 %collective-permute-done.9.got_ref = f32[2,4,8,128]{3,2,1,0:T(8,128)S(1)} collective-permute-done((f32[2,4,8,128]{3,2,1,0:T(8,128)S(1)}, f32[2,4,8,128]{3,2,1,0:T(8,128)S(1)}, u32[]{:S(2)}, u32[]{:S(2)}) %collective-permute-start.9) | collective-permute-done | bytes 32800 | tf_op jit(solution)/shard_map/ppermute | solution.py:120
  25.6 0.8 %shard_map.49 = bf16[2,7,16,256]{3,2,1,0:T(8,128)(2,1)} custom-call(f32[2,4,8,128]{3,2,1,0:T(8,128)S(1)} %get-tuple-element.14.own_ref, f32[2,4,8,128]{3,2,1,0:T(8,128)S(1)} %collective-permute-done.9.got_ref, bf16[2,7,16,256]{3,2,1,0:T(8,128)(2,1)S(1)} %get-tuple-element.16.scenes_ref), custom_call_target="tpu_custom_call" | custom-call | tf_op jit(solution)/shard_map/pallas_call | solution.py:164
  (4 shorter events, 0.1 us)
Async XLA Ops:
  1.6 7.6 %collective-permute-start.3 = (f32[8,384]{1,0:T(8,128)S(1)}, f32[8,384]{1,0:T(8,128)S(1)}, u32[]{:S(2)}, u32[]{:S(2)}) collective-permute-start(f32[8,384]{1,0:T(8,128)S(1)} %get-tuple-element.13), channel_id=1, source_target_pairs={{0,6},{1,7},{2,4},{3,5},{4,2},{5,3},{6,0},{7,1},{8,14},{9,15},{10,... | collective-permute-start | bytes 36872 | tf_op jit(solution)/shard_map/ppermute | solution.py:120
  5.7 4.2 %collective-permute-start.2 = (f32[8,384]{1,0:T(8,128)S(1)}, f32[8,384]{1,0:T(8,128)S(1)}, u32[]{:S(2)}, u32[]{:S(2)}) collective-permute-start(f32[8,384]{1,0:T(8,128)S(1)} %get-tuple-element.13), channel_id=1, source_target_pairs={{0,4},{1,5},{2,6},{3,7},{4,0},{5,1},{6,2},{7,3},{8,12},{9,13},{10,... | collective-permute-start | bytes 36872 | tf_op jit(solution)/shard_map/ppermute | solution.py:120
  6.1 3.8 %collective-permute-start.1 = (f32[8,384]{1,0:T(8,128)S(1)}, f32[8,384]{1,0:T(8,128)S(1)}, u32[]{:S(2)}, u32[]{:S(2)}) collective-permute-start(f32[8,384]{1,0:T(8,128)S(1)} %get-tuple-element.13), channel_id=1, source_target_pairs={{0,2},{1,3},{2,0},{3,1},{4,6},{5,7},{6,4},{7,5},{8,10},{9,11},{10,... | collective-permute-start | bytes 36872 | tf_op jit(solution)/shard_map/ppermute | solution.py:120
  6.3 5.2 %collective-permute-start = (bf16[2,8,8,256]{3,2,1,0:T(8,128)(2,1)S(1)}, bf16[2,8,8,256]{3,2,1,0:T(8,128)(2,1)S(1)}, u32[]{:S(2)}, u32[]{:S(2)}) collective-permute-start(bf16[2,8,8,256]{3,2,1,0:T(8,128)(2,1)S(1)} %get-tuple-element.12), channel_id=1, source_target_pairs={{0,8},{1,9},{2,10},{3,11},{4,12},{5,13},{6,14},{7,15},{8,0},{9,1},... | collective-permute-start | bytes 196616 | tf_op jit(solution)/shard_map/ppermute | solution.py:120
  9.9 1.2 %collective-permute-start.4 = (f32[8,384]{1,0:T(8,128)S(1)}, f32[8,384]{1,0:T(8,128)S(1)}, u32[]{:S(2)}, u32[]{:S(2)}) collective-permute-start(f32[8,384]{1,0:T(8,128)S(1)} %add_add_fusion), channel_id=1, source_target_pairs={{0,1},{1,0},{2,3},{3,2},{4,5},{5,4},{6,7},{7,6},{8,9},{9,8},{10,11... | collective-permute-start | bytes 36872 | tf_op jit(solution)/shard_map/ppermute | solution.py:120
  11.6 1.3 %collective-permute-start.5 = (f32[8,8,256]{2,1,0:T(8,128)S(1)}, f32[8,8,256]{2,1,0:T(8,128)S(1)}, u32[]{:S(2)}, u32[]{:S(2)}) collective-permute-start(f32[8,8,256]{2,1,0:T(8,128)S(1)} %shard_map.47), channel_id=1, source_target_pairs={{0,1},{1,0},{2,3},{3,2},{4,5},{5,4},{6,7},{7,6},{8,9},{9,8},{10,11... | collective-permute-start | bytes 196616 | tf_op jit(solution)/shard_map/ppermute | solution.py:120
  12.9 5.3 %collective-permute-start.8 = (f32[8,8,256]{2,1,0:T(8,128)S(1)}, f32[8,8,256]{2,1,0:T(8,128)S(1)}, u32[]{:S(2)}, u32[]{:S(2)}) collective-permute-start(f32[8,8,256]{2,1,0:T(8,128)S(1)} %add.19.refs_0_), channel_id=1, source_target_pairs={{0,6},{1,7},{2,4},{3,5},{4,2},{5,3},{6,0},{7,1},{8,14},{9,15},{10,... | collective-permute-start | bytes 196616 | tf_op jit(solution)/shard_map/ppermute | solution.py:120
  15.8 4.3 %collective-permute-start.7 = (f32[8,8,256]{2,1,0:T(8,128)S(1)}, f32[8,8,256]{2,1,0:T(8,128)S(1)}, u32[]{:S(2)}, u32[]{:S(2)}) collective-permute-start(f32[8,8,256]{2,1,0:T(8,128)S(1)} %add.19.refs_0_), channel_id=1, source_target_pairs={{0,4},{1,5},{2,6},{3,7},{4,0},{5,1},{6,2},{7,3},{8,12},{9,13},{10,... | collective-permute-start | bytes 196616 | tf_op jit(solution)/shard_map/ppermute | solution.py:120
  16.2 4.3 %collective-permute-start.6 = (f32[8,8,256]{2,1,0:T(8,128)S(1)}, f32[8,8,256]{2,1,0:T(8,128)S(1)}, u32[]{:S(2)}, u32[]{:S(2)}) collective-permute-start(f32[8,8,256]{2,1,0:T(8,128)S(1)} %add.19.refs_0_), channel_id=1, source_target_pairs={{0,2},{1,3},{2,0},{3,1},{4,6},{5,7},{6,4},{7,5},{8,10},{9,11},{10,... | collective-permute-start | bytes 196616 | tf_op jit(solution)/shard_map/ppermute | solution.py:120
  20.7 4.9 %collective-permute-start.9 = (f32[2,4,8,128]{3,2,1,0:T(8,128)S(1)}, f32[2,4,8,128]{3,2,1,0:T(8,128)S(1)}, u32[]{:S(2)}, u32[]{:S(2)}) collective-permute-start(f32[2,4,8,128]{3,2,1,0:T(8,128)S(1)} %get-tuple-element.15), channel_id=1, source_target_pairs={{0,8},{1,9},{2,10},{3,11},{4,12},{5,13},{6,14},{7,15},{8,0},{9,1},... | collective-permute-start | bytes 98312 | tf_op jit(solution)/shard_map/ppermute | solution.py:120

commit v3 on v0

v3 whole, which is shorter than its diff:
```python
import functools
import jax
import jax.numpy as jnp
from jax import lax
from jax.experimental import pallas as pl
from jax.experimental.pallas import tpu as pltpu
from jax.sharding import PartitionSpec as P

F32 = jnp.float32
LANES = 128
CORES = 2
VMEM = pl.BlockSpec(memory_space=pltpu.VMEM)
SMEM = pl.BlockSpec(memory_space=pltpu.SMEM)


def near(x):
    return pltpu.with_memory_space_constraint(x, pltpu.VMEM)


def chip_pairs(chips):
    half = chips // 2
    near_by = list(range(3, half + 1)) + [2]
    return list(zip(near_by, range(half + 1, chips))) + [(1, 1)]


def way_back(pairs):
    order = list(range(len(pairs)))
    return order[-2:] + order[:-2][::-1]


def place():
    me = lax.axis_index("dates")
    return me // CORES, me % CORES


def met_chip(pair):
    chip, core = place()
    return chip ^ jnp.where(core == 0, pair[0], pair[1])


def load_kernel(*refs):
    count = len(refs) // 2
    for ref, out in zip(refs[:count], refs[count:]):
        out[...] = ref[...]


def info_kernel(pif_ref, counts_ref, out_ref):
    tiles, width = out_ref.shape
    pixels = pif_ref.shape[-1]
    _, core = place()
    row = lax.broadcasted_iota(jnp.int32, (tiles, width), 0)
    count = jnp.full((tiles, LANES), counts_ref[0], jnp.int32).astype(F32)
    pif = jnp.broadcast_to(pif_ref[...], (tiles, pixels))
    out_ref[...] = jnp.where(row == core, jnp.concatenate([pif, count], axis=1), 0.0)


def pack_kernel(pairs, own_s, own_q, mate_s, mate_q, *out_refs):
    dates, bands, tiles, pixels = own_s.shape
    rows, per = bands + 1, CORES
    _, core = place()
    out_rows = len(out_refs) * rows * per
    row = lax.broadcasted_iota(jnp.int32, (out_rows, rows * tiles), 0)
    column = lax.broadcasted_iota(jnp.int32, (out_rows, rows * tiles), 1)
    slot, rest = row // (rows * per), row % (rows * per)
    target = jnp.zeros_like(row)
    for s, pair in enumerate([(0, 0)] + pairs):
        target = jnp.where(slot == s, met_chip(pair), target)
    wanted = rest // per * tiles + target * per + rest % per
    choose = (column == wanted).astype(own_s.dtype)
    for first, scenes, quality in ((core, own_s, own_q), (1 - core, mate_s, mate_q)):
        for d in range(dates):
            flat = jnp.concatenate(
                [scenes[d].reshape(bands * tiles, pixels), quality[d]], axis=0
            )
            picked = jnp.dot(choose, flat, preferred_element_type=F32)
            for s, out in enumerate(out_refs):
                block = picked[s * rows * per : (s + 1) * rows * per]
                if out.shape[0] > dates:
                    out[first * dates + d] = block.astype(out.dtype)
                elif scenes is own_s:
                    out[d] = block.astype(out.dtype)


def spread(pair_rows, rows):
    shape = (rows,) + pair_rows.shape[1:]
    row = lax.broadcasted_iota(jnp.int32, shape, 0)
    return jnp.where(
        row % CORES == 0,
        jnp.broadcast_to(pair_rows[:1], shape),
        jnp.broadcast_to(pair_rows[1:2], shape),
    )


def dates_of(pairs, refs, counts, dates):
    _, core = place()
    _, rows, pixels = refs[0].shape
    row = lax.broadcasted_iota(jnp.int32, (rows, pixels), 0)
    for s, (ref, pair) in enumerate(zip(refs, [(0, 0)] + pairs)):
        skipped = core * dates if pair[0] == pair[1] else 0
        held = []
        for j in range(ref.shape[0]):
            both = ref[j].astype(F32)
            date = met_chip(pair) * (CORES * dates) + skipped + j
            covered = (counts > date.astype(F32)).astype(F32)
            covered = jnp.concatenate([covered] * (pixels // LANES), axis=1)
            weight = both[rows - CORES :] * covered
            values = jnp.where(row < rows - CORES, both, 1.0)
            held.append((4 * (skipped + j), values, spread(weight, rows)))
        yield s, held


def partial_kernel(pairs, dates, info_ref, *refs):
    *refs, out_ref = refs
    pixels = refs[0].shape[-1]
    total = jnp.zeros(out_ref.shape, F32)
    for _, held in dates_of(pairs, refs, info_ref[:, pixels:], dates):
        for _, values, weight in held:
            total += weight * values
    out_ref[...] = total


def columns_of(terms, rows):
    lane = lax.broadcasted_iota(jnp.int32, (rows, LANES), 1)
    block = jnp.zeros((rows, LANES), F32)
    for k, term in terms:
        total = jnp.sum(term, axis=1, keepdims=True)
        block = jnp.where(lane == k, total, block)
    return block


def own_sums_kernel(pairs, dates, info_ref, *refs):
    count = len(pairs) + 1
    refs, out_refs = refs[:count], refs[count:]
    _, rows, pixels = refs[0].shape
    pif = spread(info_ref[:, :pixels], rows)
    for s, held in dates_of(pairs, refs, info_ref[:, pixels:], dates):
        terms = []
        for k, values, weight in held:
            fitted = weight * pif * values
            terms += [(k, fitted), (k + 1, fitted * values)]
        out_refs[s][...] = columns_of(terms, rows)


def cross_sums_kernel(pairs, dates, info_ref, part_ref, got_ref, *refs):
    count = len(pairs) + 1
    refs, own_refs, out_refs = refs[:count], refs[count : 2 * count], refs[2 * count :]
    _, rows, pixels = refs[0].shape
    pif = spread(info_ref[:, :pixels], rows)
    total = part_ref[...] + got_ref[...]
    composite = total / spread(total[rows - CORES :], rows)
    for s, held in dates_of(pairs, refs, info_ref[:, pixels:], dates):
        terms = []
        for k, values, weight in held:
            fit = weight * pif * composite
            terms += [(k + 2, fit), (k + 3, fit * values)]
        out_refs[s][...] = own_refs[s][...] + columns_of(terms, rows)


def sum_kernel(*refs):
    *refs, out_ref = refs
    out_ref[...] = sum(ref[...] for ref in refs)


def apply_kernel(sums_ref, got_ref, scenes_ref, out_ref):
    dates, bands, tiles, pixels = scenes_ref.shape
    _, core = place()
    sums = sums_ref[...] + got_ref[...]
    sums = jnp.where(core == 0, sums, pltpu.roll(sums, LANES - 4 * dates, 1))
    sum_x = sums + pltpu.roll(sums, sums.shape[0] - 1, 0)
    sum_xx, sum_y, sum_xy = (pltpu.roll(sum_x, LANES - k, 1) for k in (1, 2, 3))
    last = CORES * bands
    total = jnp.broadcast_to(sum_x[last : last + 1], sums.shape)
    mean_x = sum_x / total
    mean_y = sum_y / total
    spread_x = sum_xx / total - mean_x * mean_x + 1e-05
    gain = (sum_xy / total - mean_x * mean_y) / spread_x
    offset = mean_y - gain * mean_x
    for d in range(dates):
        shape = (sums.shape[0], pixels)
        slope, shift = (
            jnp.broadcast_to(x[:, 4 * d : 4 * d + 1], shape) for x in (gain, offset)
        )
        for b in range(bands):
            r = CORES * b
            values = scenes_ref[d, b].astype(F32)
            out_ref[d, b] = (slope[r : r + 1] * values + shift[r : r + 1]).astype(
                out_ref.dtype
            )


def local(size, scenes, quality, pif_mask, counts):
    dates, tiles, bands, pixels = scenes.shape
    scenes = scenes.transpose(0, 2, 1, 3)
    rows = (bands + 1) * CORES
    pairs = chip_pairs(size // CORES)

    def swap(x, near_far):
        hop = [CORES * k for k in near_far]
        return lax.ppermute(x, "dates", [(i, i ^ hop[i % CORES]) for i in range(size)])

    def mate(x):
        return lax.ppermute(x, "dates", [(i, i ^ 1) for i in range(size)])

    arguments = {id(x) for x in (scenes, quality, pif_mask, counts)}

    def call(kernel, out_shape, *args, in_specs=None):
        many = isinstance(out_shape, list)
        args = [x if id(x) in arguments else near(x) for x in args]
        return pl.pallas_call(
            kernel,
            out_shape=out_shape,
            in_specs=in_specs or [VMEM] * len(args),
            out_specs=[VMEM] * len(out_shape) if many else VMEM,
        )(*args)

    mate_scenes, mate_quality = mate(scenes), mate(quality)
    own_scenes, own_quality, own_pif = call(
        load_kernel,
        [pltpu.VMEM(x.shape, x.dtype) for x in (scenes, quality, pif_mask)],
        scenes,
        quality,
        pif_mask,
    )
    blocks = [
        pltpu.VMEM((dates * (1 if a == b else CORES), rows, pixels), scenes.dtype)
        for a, b in [(0, 0)] + pairs
    ]
    own, *sent = call(
        functools.partial(pack_kernel, pairs),
        blocks,
        own_scenes,
        own_quality,
        mate_scenes,
        mate_quality,
    )
    info = call(
        info_kernel,
        pltpu.VMEM((CORES, pixels + LANES), F32),
        own_pif,
        counts,
        in_specs=[VMEM, SMEM],
    )
    info = info + mate(info)
    held = [own] + [swap(x, pair) for x, pair in zip(sent, pairs)]
    part = call(
        functools.partial(partial_kernel, pairs, dates),
        pltpu.VMEM((rows, pixels), F32),
        info,
        *held,
    )
    sums = [pltpu.VMEM((rows, LANES), F32)] * len(held)
    own_sums = call(
        functools.partial(own_sums_kernel, pairs, dates), sums, info, *held
    )
    own, *sent = call(
        functools.partial(cross_sums_kernel, pairs, dates),
        sums,
        info,
        part,
        mate(part),
        *held,
        *own_sums,
    )
    back = [swap(sent[s], pairs[s]) for s in way_back(pairs)]
    total = call(sum_kernel, sums[0], own, *back)
    out = call(
        apply_kernel,
        jax.ShapeDtypeStruct(scenes.shape, scenes.dtype),
        total,
        mate(total),
        own_scenes,
    )
    return out.transpose(0, 2, 1, 3)


def solution(mesh):
    placed = (
        P(("groups", "dates"), None, None, None),
        P(("groups", "dates"), None, None),
        P(("groups", "dates"), None),
        P(("groups", "dates")),
    )
    return jax.shard_map(
        functools.partial(local, mesh.shape["dates"]),
        mesh=mesh,
        in_specs=placed,
        out_specs=P(("groups", "dates"), None, None, None),
        check_vma=False,
    )
```

time: 87.9 us -> 24.4 us (0.28)
  blocking collectives: 59 us -> 0 us
  local copies, waits for them, and re-layouts: 5.36 us -> 0 us
  starting transfers between devices: 11 us -> 16 us
  waiting for transfers between devices: 8.88 us -> 4.95 us
  Pallas kernels: 0 us -> 2.48 us
  other arithmetic: 1.88 us -> 0.01 us
    unnamed x1 -> x0, blocking collectives: 59 us -> none
    ppermute x0 -> x13, starting transfers between devices: none -> 16 us  [the longest x8 11.9 us: swap(): lax.ppermute(x, 'dates', [(i, i ^ hop[i % CORES]) for i in range(size)])]
    all_to_all x2 -> x0, starting transfers between devices: 11 us -> none  [the longest x1 7.39 us: local(): lax.all_to_all(quality, 'dates', split_axis=1, concat_axis=0, tiled=True)]
    all_to_all x2 -> x0, waiting for transfers between devices: 8.88 us -> none  [the longest x1 6.45 us: local(): lax.all_to_all(scenes, 'dates', split_axis=1, concat_axis=0, tiled=True)]
    ppermute x0 -> x13, waiting for transfers between devices: none -> 4.95 us  [the longest x5 2.72 us: mate(): return lax.ppermute(x, 'dates', [(i, i ^ 1) for i in range(size)])]
    unnamed x10 -> x0, local copies, waits for them, and re-layouts: 4.9 us -> none
    pallas_call x0 -> x8, Pallas kernels: none -> 2.48 us  [call(): pl.pallas_call(kernel, out_shape=out_shape, in_specs=in_specs or [VMEM] *...]
  transfers between devices with their start and end apart: 2 -> 13, of which waited for: 2 -> 7; matrix products, arithmetic and copies ran while one was open for 3% -> 0% of each run, Pallas kernels for 0% -> 5%
where the time goes in v3:
time: 24.4 us; the launch traced here: 24.2 us
  starting transfers between devices  16 us (66%)
  waiting for transfers between devices  4.95 us (20%)
  Pallas kernels  2.48 us (10%)
  between operations  0.72 us (3%)
    ppermute x8, starting transfers between devices, swap(): lax.ppermute(x, 'dates', [(i, i ^ hop[i % CORES]) for i in range(size)])  11.9 us
    ppermute x5, starting transfers between devices, mate(): return lax.ppermute(x, 'dates', [(i, i ^ 1) for i in range(size)])  4.17 us
    ppermute x5, waiting for transfers between devices, mate(): return lax.ppermute(x, 'dates', [(i, i ^ 1) for i in range(size)])  2.72 us
    pallas_call x8, Pallas kernels, call(): pl.pallas_call(kernel, out_shape=out_shape, in_specs=in_specs or [VMEM] *...  2.48 us
    ppermute x8, waiting for transfers between devices, swap(): lax.ppermute(x, 'dates', [(i, i ^ hop[i % CORES]) for i in range(size)])  2.23 us
  transfers between devices with their start and end apart: 13, of which 7 were waited for; matrix products, arithmetic and copies ran while one was open for 0% of the time, Pallas kernels for 5%

profile of v3, /device:TPU:0, one launch (start us, length us, event | category | flops | bytes accessed | tf_op | source)
XLA Modules:
  0.0 24.2 jit_solution(14465479840788669611)
XLA Ops:
  0.0 0.5 %collective-permute-start.1 = (bf16[2,7,16,256]{3,2,1,0:T(8,128)(2,1)}, bf16[2,7,16,256]{3,2,1,0:T(8,128)(2,1)S(1)}, u32[]{:S(2)}, u32[]{:S(2)}) collective-permute-start(bf16[2,7,16,256]{3,2,1,0:T(8,128)(2,1)} %bitcast.2), channel_id=1, source_target_pairs={{0,1},{1,0},{2,3},{3,2},{4,5},{5,4},{6,7},{7,6},{8,9},{9,8},{10,11... | collective-permute-start | bytes 344072 | tf_op jit(solution)/shard_map/ppermute | solution.py:202
  0.5 0.1 collective-permute-start.2
  0.5 0.9 %shard_map.46 = (bf16[2,7,16,256]{3,2,1,0:T(8,128)(2,1)S(1)}, bf16[2,16,256]{2,1,0:T(8,128)(2,1)S(1)}, f32[1,256]{1,0:T(1,128)S(1)}) custom-call(bf16[2,7,16,256]{3,2,1,0:T(8,128)(2,1)} %bitcast.3, bf16[2,16,256]{2,1,0:T(8,128)(2,1)} %refs_1_.1, f32[1,256]{1,0:T(1,128)} %refs_2_.1), custom_call_target="tpu_custom_call" | custom-call | tf_op jit(solution)/shard_map/pallas_call | solution.py:209
  1.4 0.4 %collective-permute-done.2.mate_q = bf16[2,16,256]{2,1,0:T(8,128)(2,1)S(1)} collective-permute-done((bf16[2,16,256]{2,1,0:T(8,128)(2,1)}, bf16[2,16,256]{2,1,0:T(8,128)(2,1)S(1)}, u32[]{:S(2)}, u32[]{:S(2)}) %collective-permute-start.2) | collective-permute-done | bytes 16416 | tf_op jit(solution)/shard_map/ppermute | solution.py:202
  1.8 0.0 collective-permute-done.1.mate_s
  1.9 0.2 shard_map.48
  2.0 3.8 %collective-permute-start.3 = (bf16[4,16,256]{2,1,0:T(8,128)(2,1)S(1)}, bf16[4,16,256]{2,1,0:T(8,128)(2,1)S(1)}, u32[]{:S(2)}, u32[]{:S(2)}) collective-permute-start(bf16[4,16,256]{2,1,0:T(8,128)(2,1)S(1)} %get-tuple-element.27), channel_id=1, source_target_pairs={{0,6},{1,11},{2,4},{3,9},{4,2},{5,15},{6,0},{7,13},{8,14},{9,3},{1... | collective-permute-start | bytes 98312 | tf_op jit(solution)/shard_map/ppermute | solution.py:199
  5.8 2.6 %collective-permute-start.4 = (bf16[4,16,256]{2,1,0:T(8,128)(2,1)S(1)}, bf16[4,16,256]{2,1,0:T(8,128)(2,1)S(1)}, u32[]{:S(2)}, u32[]{:S(2)}) collective-permute-start(bf16[4,16,256]{2,1,0:T(8,128)(2,1)S(1)} %get-tuple-element.28), channel_id=1, source_target_pairs={{0,8},{1,13},{2,10},{3,15},{4,12},{5,9},{6,14},{7,11},{8,0},{9,5},... | collective-permute-start | bytes 98312 | tf_op jit(solution)/shard_map/ppermute | solution.py:199
  8.4 0.4 %collective-permute-start.5 = (bf16[4,16,256]{2,1,0:T(8,128)(2,1)S(1)}, bf16[4,16,256]{2,1,0:T(8,128)(2,1)S(1)}, u32[]{:S(2)}, u32[]{:S(2)}) collective-permute-start(bf16[4,16,256]{2,1,0:T(8,128)(2,1)S(1)} %get-tuple-element.29), channel_id=1, source_target_pairs={{0,4},{1,15},{2,6},{3,13},{4,0},{5,11},{6,2},{7,9},{8,12},{9,7},{1... | collective-permute-start | bytes 98312 | tf_op jit(solution)/shard_map/ppermute | solution.py:199
  8.8 0.5 %collective-permute-start.6 = (bf16[2,16,256]{2,1,0:T(8,128)(2,1)S(1)}, bf16[2,16,256]{2,1,0:T(8,128)(2,1)S(1)}, u32[]{:S(2)}, u32[]{:S(2)}) collective-permute-start(bf16[2,16,256]{2,1,0:T(8,128)(2,1)S(1)} %get-tuple-element.30), channel_id=1, source_target_pairs={{0,2},{1,3},{2,0},{3,1},{4,6},{5,7},{6,4},{7,5},{8,10},{9,11},{10,... | collective-permute-start | bytes 49160 | tf_op jit(solution)/shard_map/ppermute | solution.py:199
  10.0 2.0 %collective-permute-start = (f32[2,384]{1,0:T(2,128)S(1)}, f32[2,384]{1,0:T(2,128)S(1)}, u32[]{:S(2)}, u32[]{:S(2)}) collective-permute-start(f32[2,384]{1,0:T(2,128)S(1)} %shard_map.47), channel_id=1, source_target_pairs={{0,1},{1,0},{2,3},{3,2},{4,5},{5,4},{6,7},{7,6},{8,9},{9,8},{10,11... | collective-permute-start | bytes 9224 | tf_op jit(solution)/shard_map/ppermute | solution.py:202
  12.1 0.8 %collective-permute-done = f32[2,384]{1,0:T(2,128)S(1)} collective-permute-done((f32[2,384]{1,0:T(2,128)S(1)}, f32[2,384]{1,0:T(2,128)S(1)}, u32[]{:S(2)}, u32[]{:S(2)}) %collective-permute-start) | collective-permute-done | bytes 3104 | tf_op jit(solution)/shard_map/ppermute | solution.py:202
  12.9 0.0 collective-permute-done.6.refs_4_
  12.9 0.0 collective-permute-done.3.refs_1_
  12.9 0.0 collective-permute-done.4.refs_2_
  12.9 0.0 collective-permute-done.5.refs_3_
  12.9 0.1 shard_map.49.part_ref
  13.0 0.5 %collective-permute-start.7 = (f32[16,256]{1,0:T(8,128)S(1)}, f32[16,256]{1,0:T(8,128)S(1)}, u32[]{:S(2)}, u32[]{:S(2)}) collective-permute-start(f32[16,256]{1,0:T(8,128)S(1)} %shard_map.49.part_ref), channel_id=1, source_target_pairs={{0,1},{1,0},{2,3},{3,2},{4,5},{5,4},{6,7},{7,6},{8,9},{9,8},{10,11... | collective-permute-start | bytes 49160 | tf_op jit(solution)/shard_map/ppermute | solution.py:202
  13.6 0.2 shard_map.50
  13.7 0.7 %collective-permute-done.7.got_ref = f32[16,256]{1,0:T(8,128)S(1)} collective-permute-done((f32[16,256]{1,0:T(8,128)S(1)}, f32[16,256]{1,0:T(8,128)S(1)}, u32[]{:S(2)}, u32[]{:S(2)}) %collective-permute-start.7) | collective-permute-done | bytes 16416 | tf_op jit(solution)/shard_map/ppermute | solution.py:202
  14.4 0.2 shard_map.51
  14.6 0.2 collective-permute-start.10
  14.8 2.8 %collective-permute-start.11 = (f32[16,128]{1,0:T(8,128)S(1)}, f32[16,128]{1,0:T(8,128)S(1)}, u32[]{:S(2)}, u32[]{:S(2)}) collective-permute-start(f32[16,128]{1,0:T(8,128)S(1)} %get-tuple-element.40), channel_id=1, source_target_pairs={{0,6},{1,11},{2,4},{3,9},{4,2},{5,15},{6,0},{7,13},{8,14},{9,3},{1... | collective-permute-start | bytes 24584 | tf_op jit(solution)/shard_map/ppermute | solution.py:199
  17.6 0.1 collective-permute-start.8
  17.7 1.5 %collective-permute-start.9 = (f32[16,128]{1,0:T(8,128)S(1)}, f32[16,128]{1,0:T(8,128)S(1)}, u32[]{:S(2)}, u32[]{:S(2)}) collective-permute-start(f32[16,128]{1,0:T(8,128)S(1)} %get-tuple-element.38), channel_id=1, source_target_pairs={{0,2},{1,3},{2,0},{3,1},{4,6},{5,7},{6,4},{7,5},{8,10},{9,11},{10,... | collective-permute-start | bytes 24584 | tf_op jit(solution)/shard_map/ppermute | solution.py:199
  19.1 0.0 collective-permute-done.10.refs_3_
  19.2 0.2 collective-permute-done.11.refs_4_
  19.3 1.9 %collective-permute-done.8.refs_1_ = f32[16,128]{1,0:T(8,128)S(1)} collective-permute-done((f32[16,128]{1,0:T(8,128)S(1)}, f32[16,128]{1,0:T(8,128)S(1)}, u32[]{:S(2)}, u32[]{:S(2)}) %collective-permute-start.8) | collective-permute-done | bytes 8224 | tf_op jit(solution)/shard_map/ppermute | solution.py:199
  21.3 0.1 collective-permute-done.9.refs_2_
  21.4 1.1 %collective-permute-start.12 = (f32[16,128]{1,0:T(8,128)S(1)}, f32[16,128]{1,0:T(8,128)S(1)}, u32[]{:S(2)}, u32[]{:S(2)}) collective-permute-start(f32[16,128]{1,0:T(8,128)S(1)} %shard_map.52.sums_ref), channel_id=1, source_target_pairs={{0,1},{1,0},{2,3},{3,2},{4,5},{5,4},{6,7},{7,6},{8,9},{9,8},{10,11... | collective-permute-start | bytes 24584 | tf_op jit(solution)/shard_map/ppermute | solution.py:202
  22.5 0.8 %collective-permute-done.12.got_ref = f32[16,128]{1,0:T(8,128)S(1)} collective-permute-done((f32[16,128]{1,0:T(8,128)S(1)}, f32[16,128]{1,0:T(8,128)S(1)}, u32[]{:S(2)}, u32[]{:S(2)}) %collective-permute-start.12) | collective-permute-done | bytes 8224 | tf_op jit(solution)/shard_map/ppermute | solution.py:202
  23.3 0.9 %shard_map.53 = bf16[2,7,16,256]{3,2,1,0:T(8,128)(2,1)} custom-call(f32[16,128]{1,0:T(8,128)S(1)} %shard_map.52.sums_ref, f32[16,128]{1,0:T(8,128)S(1)} %collective-permute-done.12.got_ref, bf16[2,7,16,256]{3,2,1,0:T(8,128)(2,1)S(1)} %get-tuple-element.24.own_s.scenes_ref), custom_call_target="tpu_custom_call" | custom-call | tf_op jit(solution)/shard_map/pallas_call | solution.py:209
  (3 shorter events, 0.0 us)
Async XLA Ops:
  0.0 1.9 %collective-permute-start.1 = (bf16[2,7,16,256]{3,2,1,0:T(8,128)(2,1)}, bf16[2,7,16,256]{3,2,1,0:T(8,128)(2,1)S(1)}, u32[]{:S(2)}, u32[]{:S(2)}) collective-permute-start(bf16[2,7,16,256]{3,2,1,0:T(8,128)(2,1)} %bitcast.2), channel_id=1, source_target_pairs={{0,1},{1,0},{2,3},{3,2},{4,5},{5,4},{6,7},{7,6},{8,9},{9,8},{10,11... | collective-permute-start | bytes 344072 | tf_op jit(solution)/shard_map/ppermute | solution.py:202
  0.5 1.4 %collective-permute-start.2 = (bf16[2,16,256]{2,1,0:T(8,128)(2,1)}, bf16[2,16,256]{2,1,0:T(8,128)(2,1)S(1)}, u32[]{:S(2)}, u32[]{:S(2)}) collective-permute-start(bf16[2,16,256]{2,1,0:T(8,128)(2,1)} %refs_1_.1), channel_id=1, source_target_pairs={{0,1},{1,0},{2,3},{3,2},{4,5},{5,4},{6,7},{7,6},{8,9},{9,8},{10,11... | collective-permute-start | bytes 49160 | tf_op jit(solution)/shard_map/ppermute | solution.py:202
  2.0 10.9 %collective-permute-start.3 = (bf16[4,16,256]{2,1,0:T(8,128)(2,1)S(1)}, bf16[4,16,256]{2,1,0:T(8,128)(2,1)S(1)}, u32[]{:S(2)}, u32[]{:S(2)}) collective-permute-start(bf16[4,16,256]{2,1,0:T(8,128)(2,1)S(1)} %get-tuple-element.27), channel_id=1, source_target_pairs={{0,6},{1,11},{2,4},{3,9},{4,2},{5,15},{6,0},{7,13},{8,14},{9,3},{1... | collective-permute-start | bytes 98312 | tf_op jit(solution)/shard_map/ppermute | solution.py:199
  5.8 7.1 %collective-permute-start.4 = (bf16[4,16,256]{2,1,0:T(8,128)(2,1)S(1)}, bf16[4,16,256]{2,1,0:T(8,128)(2,1)S(1)}, u32[]{:S(2)}, u32[]{:S(2)}) collective-permute-start(bf16[4,16,256]{2,1,0:T(8,128)(2,1)S(1)} %get-tuple-element.28), channel_id=1, source_target_pairs={{0,8},{1,13},{2,10},{3,15},{4,12},{5,9},{6,14},{7,11},{8,0},{9,5},... | collective-permute-start | bytes 98312 | tf_op jit(solution)/shard_map/ppermute | solution.py:199
  8.4 4.5 %collective-permute-start.5 = (bf16[4,16,256]{2,1,0:T(8,128)(2,1)S(1)}, bf16[4,16,256]{2,1,0:T(8,128)(2,1)S(1)}, u32[]{:S(2)}, u32[]{:S(2)}) collective-permute-start(bf16[4,16,256]{2,1,0:T(8,128)(2,1)S(1)} %get-tuple-element.29), channel_id=1, source_target_pairs={{0,4},{1,15},{2,6},{3,13},{4,0},{5,11},{6,2},{7,9},{8,12},{9,7},{1... | collective-permute-start | bytes 98312 | tf_op jit(solution)/shard_map/ppermute | solution.py:199
  8.8 4.1 %collective-permute-start.6 = (bf16[2,16,256]{2,1,0:T(8,128)(2,1)S(1)}, bf16[2,16,256]{2,1,0:T(8,128)(2,1)S(1)}, u32[]{:S(2)}, u32[]{:S(2)}) collective-permute-start(bf16[2,16,256]{2,1,0:T(8,128)(2,1)S(1)} %get-tuple-element.30), channel_id=1, source_target_pairs={{0,2},{1,3},{2,0},{3,1},{4,6},{5,7},{6,4},{7,5},{8,10},{9,11},{10,... | collective-permute-start | bytes 49160 | tf_op jit(solution)/shard_map/ppermute | solution.py:199
  10.0 2.9 %collective-permute-start = (f32[2,384]{1,0:T(2,128)S(1)}, f32[2,384]{1,0:T(2,128)S(1)}, u32[]{:S(2)}, u32[]{:S(2)}) collective-permute-start(f32[2,384]{1,0:T(2,128)S(1)} %shard_map.47), channel_id=1, source_target_pairs={{0,1},{1,0},{2,3},{3,2},{4,5},{5,4},{6,7},{7,6},{8,9},{9,8},{10,11... | collective-permute-start | bytes 9224 | tf_op jit(solution)/shard_map/ppermute | solution.py:202
  13.0 1.4 %collective-permute-start.7 = (f32[16,256]{1,0:T(8,128)S(1)}, f32[16,256]{1,0:T(8,128)S(1)}, u32[]{:S(2)}, u32[]{:S(2)}) collective-permute-start(f32[16,256]{1,0:T(8,128)S(1)} %shard_map.49.part_ref), channel_id=1, source_target_pairs={{0,1},{1,0},{2,3},{3,2},{4,5},{5,4},{6,7},{7,6},{8,9},{9,8},{10,11... | collective-permute-start | bytes 49160 | tf_op jit(solution)/shard_map/ppermute | solution.py:202
  14.6 4.6 %collective-permute-start.10 = (f32[16,128]{1,0:T(8,128)S(1)}, f32[16,128]{1,0:T(8,128)S(1)}, u32[]{:S(2)}, u32[]{:S(2)}) collective-permute-start(f32[16,128]{1,0:T(8,128)S(1)} %get-tuple-element.39), channel_id=1, source_target_pairs={{0,8},{1,13},{2,10},{3,15},{4,12},{5,9},{6,14},{7,11},{8,0},{9,5},... | collective-permute-start | bytes 24584 | tf_op jit(solution)/shard_map/ppermute | solution.py:199
  14.8 4.5 %collective-permute-start.11 = (f32[16,128]{1,0:T(8,128)S(1)}, f32[16,128]{1,0:T(8,128)S(1)}, u32[]{:S(2)}, u32[]{:S(2)}) collective-permute-start(f32[16,128]{1,0:T(8,128)S(1)} %get-tuple-element.40), channel_id=1, source_target_pairs={{0,6},{1,11},{2,4},{3,9},{4,2},{5,15},{6,0},{7,13},{8,14},{9,3},{1... | collective-permute-start | bytes 24584 | tf_op jit(solution)/shard_map/ppermute | solution.py:199
  17.6 3.7 %collective-permute-start.8 = (f32[16,128]{1,0:T(8,128)S(1)}, f32[16,128]{1,0:T(8,128)S(1)}, u32[]{:S(2)}, u32[]{:S(2)}) collective-permute-start(f32[16,128]{1,0:T(8,128)S(1)} %get-tuple-element.37), channel_id=1, source_target_pairs={{0,4},{1,15},{2,6},{3,13},{4,0},{5,11},{6,2},{7,9},{8,12},{9,7},{1... | collective-permute-start | bytes 24584 | tf_op jit(solution)/shard_map/ppermute | solution.py:199
  17.7 3.7 %collective-permute-start.9 = (f32[16,128]{1,0:T(8,128)S(1)}, f32[16,128]{1,0:T(8,128)S(1)}, u32[]{:S(2)}, u32[]{:S(2)}) collective-permute-start(f32[16,128]{1,0:T(8,128)S(1)} %get-tuple-element.38), channel_id=1, source_target_pairs={{0,2},{1,3},{2,0},{3,1},{4,6},{5,7},{6,4},{7,5},{8,10},{9,11},{10,... | collective-permute-start | bytes 24584 | tf_op jit(solution)/shard_map/ppermute | solution.py:199
  21.4 1.9 %collective-permute-start.12 = (f32[16,128]{1,0:T(8,128)S(1)}, f32[16,128]{1,0:T(8,128)S(1)}, u32[]{:S(2)}, u32[]{:S(2)}) collective-permute-start(f32[16,128]{1,0:T(8,128)S(1)} %shard_map.52.sums_ref), channel_id=1, source_target_pairs={{0,1},{1,0},{2,3},{3,2},{4,5},{5,4},{6,7},{7,6},{8,9},{9,8},{10,11... | collective-permute-start | bytes 24584 | tf_op jit(solution)/shard_map/ppermute | solution.py:202

commit v4 on v3

--- a/solution.py
+++ b/solution.py
@@ -18,14 +18,14 @@
 
 
 def chip_pairs(chips):
-    half = chips // 2
-    near_by = list(range(3, half + 1)) + [2]
-    return list(zip(near_by, range(half + 1, chips))) + [(1, 1)]
+    odd = list(range(3, chips, 2))
+    return list(zip(range(chips - 2, 0, -2), odd[1:] + odd[:1])) + [(1, 1)]
 
 
 def way_back(pairs):
-    order = list(range(len(pairs)))
-    return order[-2:] + order[:-2][::-1]
+    couples = sorted((a, a + 1) for a, b in pairs if a != b)
+    first = couples.pop(len(couples) // 2) if couples else (1, 1)
+    return [first] + [(1, 1)] * bool(pairs[1:]) + couples
 
 
 def place():
@@ -148,12 +148,19 @@
     pif = spread(info_ref[:, :pixels], rows)
     total = part_ref[...] + got_ref[...]
     composite = total / spread(total[rows - CORES :], rows)
+    blocks = []
     for s, held in dates_of(pairs, refs, info_ref[:, pixels:], dates):
         terms = []
         for k, values, weight in held:
             fit = weight * pif * composite
             terms += [(k + 2, fit), (k + 3, fit * values)]
-        out_refs[s][...] = own_refs[s][...] + columns_of(terms, rows)
+        blocks.append(own_refs[s][...] + columns_of(terms, rows))
+    _, core = place()
+    out_refs[0][...] = blocks[0]
+    near_by, far_off = zip(*pairs)
+    for out, (a, b) in zip(out_refs[1:], way_back(pairs)):
+        first, second = near_by.index(a) + 1, far_off.index(b) + 1
+        out[...] = jnp.where(core == 0, blocks[first], blocks[second])
 
 
 def sum_kernel(*refs):
@@ -161,11 +168,10 @@
     out_ref[...] = sum(ref[...] for ref in refs)
 
 
-def apply_kernel(sums_ref, got_ref, scenes_ref, out_ref):
+def apply_kernel(sums_ref, got_ref, scenes_ref, out_ref, done_ref, sems):
     dates, bands, tiles, pixels = scenes_ref.shape
     _, core = place()
     sums = sums_ref[...] + got_ref[...]
-    sums = jnp.where(core == 0, sums, pltpu.roll(sums, LANES - 4 * dates, 1))
     sum_x = sums + pltpu.roll(sums, sums.shape[0] - 1, 0)
     sum_xx, sum_y, sum_xy = (pltpu.roll(sum_x, LANES - k, 1) for k in (1, 2, 3))
     last = CORES * bands
@@ -175,17 +181,27 @@
     spread_x = sum_xx / total - mean_x * mean_x + 1e-05
     gain = (sum_xy / total - mean_x * mean_y) / spread_x
     offset = mean_y - gain * mean_x
+    copies = []
     for d in range(dates):
         shape = (sums.shape[0], pixels)
         slope, shift = (
-            jnp.broadcast_to(x[:, 4 * d : 4 * d + 1], shape) for x in (gain, offset)
+            jnp.where(
+                core == 0,
+                jnp.broadcast_to(x[:, 4 * d : 4 * d + 1], shape),
+                jnp.broadcast_to(x[:, 4 * (d + dates) : 4 * (d + dates) + 1], shape),
+            )
+            for x in (gain, offset)
         )
         for b in range(bands):
             r = CORES * b
             values = scenes_ref[d, b].astype(F32)
-            out_ref[d, b] = (slope[r : r + 1] * values + shift[r : r + 1]).astype(
-                out_ref.dtype
+            done_ref[d, b] = (slope[r : r + 1] * values + shift[r : r + 1]).astype(
+                done_ref.dtype
             )
+        copies.append(pltpu.make_async_copy(done_ref.at[d], out_ref.at[d], sems.at[d]))
+        copies[-1].start()
+    for copy in copies:
+        copy.wait()
 
 
 def local(size, scenes, quality, pif_mask, counts):
@@ -261,15 +277,18 @@
         *held,
         *own_sums,
     )
-    back = [swap(sent[s], pairs[s]) for s in way_back(pairs)]
+    back = [swap(x, pair) for x, pair in zip(sent, way_back(pairs))]
     total = call(sum_kernel, sums[0], own, *back)
-    out = call(
+    out = pl.pallas_call(
         apply_kernel,
-        jax.ShapeDtypeStruct(scenes.shape, scenes.dtype),
-        total,
-        mate(total),
-        own_scenes,
-    )
+        out_shape=jax.ShapeDtypeStruct(scenes.shape, scenes.dtype),
+        in_specs=[VMEM] * 3,
+        out_specs=pl.BlockSpec(memory_space=pl.ANY),
+        scratch_shapes=[
+            pltpu.VMEM(scenes.shape, scenes.dtype),
+            pltpu.SemaphoreType.DMA((dates,)),
+        ],
+    )(near(total), near(mate(total)), near(own_scenes))
     return out.transpose(0, 2, 1, 3)
 
 

time: 24.4 us -> 23.8 us (0.975)
  starting transfers between devices: 16 us -> 14 us
  waiting for transfers between devices: 4.95 us -> 6.54 us
    ppermute x5, starting transfers between devices: 4.17 us -> 1.73 us  [mate(): return lax.ppermute(x, 'dates', [(i, i ^ 1) for i in range(size)])]
    ppermute x8, waiting for transfers between devices: 2.23 us -> 3.66 us  [swap(): lax.ppermute(x, 'dates', [(i, i ^ hop[i % CORES]) for i in range(size)])]
    pallas_call x8 -> x7, Pallas kernels: 2.48 us -> 1.55 us  [call(): pl.pallas_call(kernel, out_shape=out_shape, in_specs=in_specs or [VMEM] *...]
    pallas_call x0 -> x1, Pallas kernels: none -> 0.84 us  [local(): pl.pallas_call(apply_kernel, out_shape=jax.ShapeDtypeStruct(scenes.shape,...]
    ppermute x8, starting transfers between devices: 11.9 us -> 12.3 us  [swap(): lax.ppermute(x, 'dates', [(i, i ^ hop[i % CORES]) for i in range(size)])]
  transfers between devices with their start and end apart: 13 -> 13, of which waited for: 7 -> 8; matrix products, arithmetic and copies ran while one was open for 0% -> 0% of each run, Pallas kernels for 5% -> 5%
where the time goes in v4:
time: 23.8 us; the launch traced here: 23.7 us
  starting transfers between devices  14 us (59%)
  waiting for transfers between devices  6.54 us (27%)
  Pallas kernels  2.39 us (10%)
  between operations  0.71 us (3%)
    ppermute x8, starting transfers between devices, swap(): lax.ppermute(x, 'dates', [(i, i ^ hop[i % CORES]) for i in range(size)])  12.3 us
    ppermute x8, waiting for transfers between devices, swap(): lax.ppermute(x, 'dates', [(i, i ^ hop[i % CORES]) for i in range(size)])  3.66 us
    ppermute x5, waiting for transfers between devices, mate(): return lax.ppermute(x, 'dates', [(i, i ^ 1) for i in range(size)])  2.88 us
    ppermute x5, starting transfers between devices, mate(): return lax.ppermute(x, 'dates', [(i, i ^ 1) for i in range(size)])  1.73 us
    pallas_call x7, Pallas kernels, call(): pl.pallas_call(kernel, out_shape=out_shape, in_specs=in_specs or [VMEM] *...  1.55 us
    pallas_call x1, Pallas kernels, local(): pl.pallas_call(apply_kernel, out_shape=jax.ShapeDtypeStruct(scenes.shape,...  0.84 us
  transfers between devices with their start and end apart: 13, of which 8 were waited for; matrix products, arithmetic and copies ran while one was open for 0% of the time, Pallas kernels for 5%

profile of v4, /device:TPU:0, one launch (start us, length us, event | category | flops | bytes accessed | tf_op | source)
XLA Modules:
  0.0 23.7 jit_solution(13714920016530605973)
XLA Ops:
  0.0 0.5 %collective-permute-start.1 = (bf16[2,7,16,256]{3,2,1,0:T(8,128)(2,1)}, bf16[2,7,16,256]{3,2,1,0:T(8,128)(2,1)S(1)}, u32[]{:S(2)}, u32[]{:S(2)}) collective-permute-start(bf16[2,7,16,256]{3,2,1,0:T(8,128)(2,1)} %bitcast.2), channel_id=1, source_target_pairs={{0,1},{1,0},{2,3},{3,2},{4,5},{5,4},{6,7},{7,6},{8,9},{9,8},{10,11... | collective-permute-start | bytes 344072 | tf_op jit(solution)/shard_map/ppermute | solution.py:218
  0.5 0.1 collective-permute-start.2
  0.5 0.9 %shard_map.46 = (bf16[2,7,16,256]{3,2,1,0:T(8,128)(2,1)S(1)}, bf16[2,16,256]{2,1,0:T(8,128)(2,1)S(1)}, f32[1,256]{1,0:T(1,128)S(1)}) custom-call(bf16[2,7,16,256]{3,2,1,0:T(8,128)(2,1)} %bitcast.3, bf16[2,16,256]{2,1,0:T(8,128)(2,1)} %refs_1_.1, f32[1,256]{1,0:T(1,128)} %refs_2_.1), custom_call_target="tpu_custom_call" | custom-call | tf_op jit(solution)/shard_map/pallas_call | solution.py:225
  1.4 0.4 %collective-permute-done.2.mate_q = bf16[2,16,256]{2,1,0:T(8,128)(2,1)S(1)} collective-permute-done((bf16[2,16,256]{2,1,0:T(8,128)(2,1)}, bf16[2,16,256]{2,1,0:T(8,128)(2,1)S(1)}, u32[]{:S(2)}, u32[]{:S(2)}) %collective-permute-start.2) | collective-permute-done | bytes 16416 | tf_op jit(solution)/shard_map/ppermute | solution.py:218
  1.8 0.0 collective-permute-done.1.mate_s
  1.9 0.2 shard_map.48
  2.0 4.8 %collective-permute-start.3 = (bf16[4,16,256]{2,1,0:T(8,128)(2,1)S(1)}, bf16[4,16,256]{2,1,0:T(8,128)(2,1)S(1)}, u32[]{:S(2)}, u32[]{:S(2)}) collective-permute-start(bf16[4,16,256]{2,1,0:T(8,128)(2,1)S(1)} %get-tuple-element.27), channel_id=1, source_target_pairs={{0,12},{1,11},{2,14},{3,9},{4,8},{5,15},{6,10},{7,13},{8,4},{9,3},... | collective-permute-start | bytes 98312 | tf_op jit(solution)/shard_map/ppermute | solution.py:215
  6.9 0.0 collective-permute-start.4
  6.9 0.6 %collective-permute-start.5 = (bf16[4,16,256]{2,1,0:T(8,128)(2,1)S(1)}, bf16[4,16,256]{2,1,0:T(8,128)(2,1)S(1)}, u32[]{:S(2)}, u32[]{:S(2)}) collective-permute-start(bf16[4,16,256]{2,1,0:T(8,128)(2,1)S(1)} %get-tuple-element.29), channel_id=1, source_target_pairs={{0,4},{1,7},{2,6},{3,5},{4,0},{5,3},{6,2},{7,1},{8,12},{9,15},{10,... | collective-permute-start | bytes 98312 | tf_op jit(solution)/shard_map/ppermute | solution.py:215
  7.5 1.7 %collective-permute-start.6 = (bf16[2,16,256]{2,1,0:T(8,128)(2,1)S(1)}, bf16[2,16,256]{2,1,0:T(8,128)(2,1)S(1)}, u32[]{:S(2)}, u32[]{:S(2)}) collective-permute-start(bf16[2,16,256]{2,1,0:T(8,128)(2,1)S(1)} %get-tuple-element.30), channel_id=1, source_target_pairs={{0,2},{1,3},{2,0},{3,1},{4,6},{5,7},{6,4},{7,5},{8,10},{9,11},{10,... | collective-permute-start | bytes 49160 | tf_op jit(solution)/shard_map/ppermute | solution.py:215
  9.8 0.2 %collective-permute-start = (f32[2,384]{1,0:T(2,128)S(1)}, f32[2,384]{1,0:T(2,128)S(1)}, u32[]{:S(2)}, u32[]{:S(2)}) collective-permute-start(f32[2,384]{1,0:T(2,128)S(1)} %shard_map.47), channel_id=1, source_target_pairs={{0,1},{1,0},{2,3},{3,2},{4,5},{5,4},{6,7},{7,6},{8,9},{9,8},{10,11... | collective-permute-start | bytes 9224 | tf_op jit(solution)/shard_map/ppermute | solution.py:218
  10.1 1.0 %collective-permute-done = f32[2,384]{1,0:T(2,128)S(1)} collective-permute-done((f32[2,384]{1,0:T(2,128)S(1)}, f32[2,384]{1,0:T(2,128)S(1)}, u32[]{:S(2)}, u32[]{:S(2)}) %collective-permute-start) | collective-permute-done | bytes 3104 | tf_op jit(solution)/shard_map/ppermute | solution.py:218
  11.1 0.2 collective-permute-done.6.refs_4_
  11.2 0.0 collective-permute-done.3.refs_1_
  11.3 0.7 %collective-permute-done.4.refs_2_ = bf16[4,16,256]{2,1,0:T(8,128)(2,1)S(1)} collective-permute-done((bf16[4,16,256]{2,1,0:T(8,128)(2,1)S(1)}, bf16[4,16,256]{2,1,0:T(8,128)(2,1)S(1)}, u32[]{:S(2)}, u32[]{:S(2)}) %collective-permute-start.4) | collective-permute-done | bytes 32800 | tf_op jit(solution)/shard_map/ppermute | solution.py:215
  12.0 0.0 collective-permute-done.5.refs_3_
  12.0 0.1 shard_map.49.part_ref
  12.1 0.5 %collective-permute-start.7 = (f32[16,256]{1,0:T(8,128)S(1)}, f32[16,256]{1,0:T(8,128)S(1)}, u32[]{:S(2)}, u32[]{:S(2)}) collective-permute-start(f32[16,256]{1,0:T(8,128)S(1)} %shard_map.49.part_ref), channel_id=1, source_target_pairs={{0,1},{1,0},{2,3},{3,2},{4,5},{5,4},{6,7},{7,6},{8,9},{9,8},{10,11... | collective-permute-start | bytes 49160 | tf_op jit(solution)/shard_map/ppermute | solution.py:218
  12.5 0.2 shard_map.50
  12.7 0.7 %collective-permute-done.7.got_ref = f32[16,256]{1,0:T(8,128)S(1)} collective-permute-done((f32[16,256]{1,0:T(8,128)S(1)}, f32[16,256]{1,0:T(8,128)S(1)}, u32[]{:S(2)}, u32[]{:S(2)}) %collective-permute-start.7) | collective-permute-done | bytes 16416 | tf_op jit(solution)/shard_map/ppermute | solution.py:218
  13.4 0.2 shard_map.51
  13.5 1.1 %collective-permute-start.10 = (f32[16,128]{1,0:T(8,128)S(1)}, f32[16,128]{1,0:T(8,128)S(1)}, u32[]{:S(2)}, u32[]{:S(2)}) collective-permute-start(f32[16,128]{1,0:T(8,128)S(1)} %get-tuple-element.39), channel_id=1, source_target_pairs={{0,4},{1,7},{2,6},{3,5},{4,0},{5,3},{6,2},{7,1},{8,12},{9,15},{10,... | collective-permute-start | bytes 24584 | tf_op jit(solution)/shard_map/ppermute | solution.py:215
  14.6 2.3 %collective-permute-start.11 = (f32[16,128]{1,0:T(8,128)S(1)}, f32[16,128]{1,0:T(8,128)S(1)}, u32[]{:S(2)}, u32[]{:S(2)}) collective-permute-start(f32[16,128]{1,0:T(8,128)S(1)} %get-tuple-element.40), channel_id=1, source_target_pairs={{0,12},{1,15},{2,14},{3,13},{4,8},{5,11},{6,10},{7,9},{8,4},{9,7},... | collective-permute-start | bytes 24584 | tf_op jit(solution)/shard_map/ppermute | solution.py:215
  16.9 0.3 %collective-permute-start.8 = (f32[16,128]{1,0:T(8,128)S(1)}, f32[16,128]{1,0:T(8,128)S(1)}, u32[]{:S(2)}, u32[]{:S(2)}) collective-permute-start(f32[16,128]{1,0:T(8,128)S(1)} %get-tuple-element.37), channel_id=1, source_target_pairs={{0,8},{1,11},{2,10},{3,9},{4,12},{5,15},{6,14},{7,13},{8,0},{9,3},... | collective-permute-start | bytes 24584 | tf_op jit(solution)/shard_map/ppermute | solution.py:215
  17.2 1.5 %collective-permute-start.9 = (f32[16,128]{1,0:T(8,128)S(1)}, f32[16,128]{1,0:T(8,128)S(1)}, u32[]{:S(2)}, u32[]{:S(2)}) collective-permute-start(f32[16,128]{1,0:T(8,128)S(1)} %get-tuple-element.38), channel_id=1, source_target_pairs={{0,2},{1,3},{2,0},{3,1},{4,6},{5,7},{6,4},{7,5},{8,10},{9,11},{10,... | collective-permute-start | bytes 24584 | tf_op jit(solution)/shard_map/ppermute | solution.py:215
  18.7 0.0 collective-permute-done.10.refs_3_
  18.7 1.4 %collective-permute-done.11.refs_4_ = f32[16,128]{1,0:T(8,128)S(1)} collective-permute-done((f32[16,128]{1,0:T(8,128)S(1)}, f32[16,128]{1,0:T(8,128)S(1)}, u32[]{:S(2)}, u32[]{:S(2)}) %collective-permute-start.11) | collective-permute-done | bytes 8224 | tf_op jit(solution)/shard_map/ppermute | solution.py:215
  20.1 1.4 %collective-permute-done.8.refs_1_ = f32[16,128]{1,0:T(8,128)S(1)} collective-permute-done((f32[16,128]{1,0:T(8,128)S(1)}, f32[16,128]{1,0:T(8,128)S(1)}, u32[]{:S(2)}, u32[]{:S(2)}) %collective-permute-start.8) | collective-permute-done | bytes 8224 | tf_op jit(solution)/shard_map/ppermute | solution.py:215
  21.5 0.0 collective-permute-done.9.refs_2_
  21.5 0.5 %collective-permute-start.12 = (f32[16,128]{1,0:T(8,128)S(1)}, f32[16,128]{1,0:T(8,128)S(1)}, u32[]{:S(2)}, u32[]{:S(2)}) collective-permute-start(f32[16,128]{1,0:T(8,128)S(1)} %shard_map.52.sums_ref), channel_id=1, source_target_pairs={{0,1},{1,0},{2,3},{3,2},{4,5},{5,4},{6,7},{7,6},{8,9},{9,8},{10,11... | collective-permute-start | bytes 24584 | tf_op jit(solution)/shard_map/ppermute | solution.py:218
  22.0 0.8 %collective-permute-done.12.got_ref = f32[16,128]{1,0:T(8,128)S(1)} collective-permute-done((f32[16,128]{1,0:T(8,128)S(1)}, f32[16,128]{1,0:T(8,128)S(1)}, u32[]{:S(2)}, u32[]{:S(2)}) %collective-permute-start.12) | collective-permute-done | bytes 8224 | tf_op jit(solution)/shard_map/ppermute | solution.py:218
  22.8 0.8 %shard_map.53 = bf16[2,7,16,256]{3,2,1,0:T(8,128)(2,1)} custom-call(f32[16,128]{1,0:T(8,128)S(1)} %shard_map.52.sums_ref, f32[16,128]{1,0:T(8,128)S(1)} %collective-permute-done.12.got_ref, bf16[2,7,16,256]{3,2,1,0:T(8,128)(2,1)S(1)} %get-tuple-element.24.own_s.scenes_ref), custom_call_target="tpu_custom_call" | custom-call | tf_op jit(solution)/shard_map/pallas_call | solution.py:282
  (3 shorter events, 0.0 us)
Async XLA Ops:
  0.0 1.9 %collective-permute-start.1 = (bf16[2,7,16,256]{3,2,1,0:T(8,128)(2,1)}, bf16[2,7,16,256]{3,2,1,0:T(8,128)(2,1)S(1)}, u32[]{:S(2)}, u32[]{:S(2)}) collective-permute-start(bf16[2,7,16,256]{3,2,1,0:T(8,128)(2,1)} %bitcast.2), channel_id=1, source_target_pairs={{0,1},{1,0},{2,3},{3,2},{4,5},{5,4},{6,7},{7,6},{8,9},{9,8},{10,11... | collective-permute-start | bytes 344072 | tf_op jit(solution)/shard_map/ppermute | solution.py:218
  0.5 1.4 %collective-permute-start.2 = (bf16[2,16,256]{2,1,0:T(8,128)(2,1)}, bf16[2,16,256]{2,1,0:T(8,128)(2,1)S(1)}, u32[]{:S(2)}, u32[]{:S(2)}) collective-permute-start(bf16[2,16,256]{2,1,0:T(8,128)(2,1)} %refs_1_.1), channel_id=1, source_target_pairs={{0,1},{1,0},{2,3},{3,2},{4,5},{5,4},{6,7},{7,6},{8,9},{9,8},{10,11... | collective-permute-start | bytes 49160 | tf_op jit(solution)/shard_map/ppermute | solution.py:218
  2.0 9.2 %collective-permute-start.3 = (bf16[4,16,256]{2,1,0:T(8,128)(2,1)S(1)}, bf16[4,16,256]{2,1,0:T(8,128)(2,1)S(1)}, u32[]{:S(2)}, u32[]{:S(2)}) collective-permute-start(bf16[4,16,256]{2,1,0:T(8,128)(2,1)S(1)} %get-tuple-element.27), channel_id=1, source_target_pairs={{0,12},{1,11},{2,14},{3,9},{4,8},{5,15},{6,10},{7,13},{8,4},{9,3},... | collective-permute-start | bytes 98312 | tf_op jit(solution)/shard_map/ppermute | solution.py:215
  6.9 5.1 %collective-permute-start.4 = (bf16[4,16,256]{2,1,0:T(8,128)(2,1)S(1)}, bf16[4,16,256]{2,1,0:T(8,128)(2,1)S(1)}, u32[]{:S(2)}, u32[]{:S(2)}) collective-permute-start(bf16[4,16,256]{2,1,0:T(8,128)(2,1)S(1)} %get-tuple-element.28), channel_id=1, source_target_pairs={{0,8},{1,15},{2,10},{3,13},{4,12},{5,11},{6,14},{7,9},{8,0},{9,7},... | collective-permute-start | bytes 98312 | tf_op jit(solution)/shard_map/ppermute | solution.py:215
  6.9 5.1 %collective-permute-start.5 = (bf16[4,16,256]{2,1,0:T(8,128)(2,1)S(1)}, bf16[4,16,256]{2,1,0:T(8,128)(2,1)S(1)}, u32[]{:S(2)}, u32[]{:S(2)}) collective-permute-start(bf16[4,16,256]{2,1,0:T(8,128)(2,1)S(1)} %get-tuple-element.29), channel_id=1, source_target_pairs={{0,4},{1,7},{2,6},{3,5},{4,0},{5,3},{6,2},{7,1},{8,12},{9,15},{10,... | collective-permute-start | bytes 98312 | tf_op jit(solution)/shard_map/ppermute | solution.py:215
  7.5 3.7 %collective-permute-start.6 = (bf16[2,16,256]{2,1,0:T(8,128)(2,1)S(1)}, bf16[2,16,256]{2,1,0:T(8,128)(2,1)S(1)}, u32[]{:S(2)}, u32[]{:S(2)}) collective-permute-start(bf16[2,16,256]{2,1,0:T(8,128)(2,1)S(1)} %get-tuple-element.30), channel_id=1, source_target_pairs={{0,2},{1,3},{2,0},{3,1},{4,6},{5,7},{6,4},{7,5},{8,10},{9,11},{10,... | collective-permute-start | bytes 49160 | tf_op jit(solution)/shard_map/ppermute | solution.py:215
  9.8 1.2 %collective-permute-start = (f32[2,384]{1,0:T(2,128)S(1)}, f32[2,384]{1,0:T(2,128)S(1)}, u32[]{:S(2)}, u32[]{:S(2)}) collective-permute-start(f32[2,384]{1,0:T(2,128)S(1)} %shard_map.47), channel_id=1, source_target_pairs={{0,1},{1,0},{2,3},{3,2},{4,5},{5,4},{6,7},{7,6},{8,9},{9,8},{10,11... | collective-permute-start | bytes 9224 | tf_op jit(solution)/shard_map/ppermute | solution.py:218
  12.1 1.3 %collective-permute-start.7 = (f32[16,256]{1,0:T(8,128)S(1)}, f32[16,256]{1,0:T(8,128)S(1)}, u32[]{:S(2)}, u32[]{:S(2)}) collective-permute-start(f32[16,256]{1,0:T(8,128)S(1)} %shard_map.49.part_ref), channel_id=1, source_target_pairs={{0,1},{1,0},{2,3},{3,2},{4,5},{5,4},{6,7},{7,6},{8,9},{9,8},{10,11... | collective-permute-start | bytes 49160 | tf_op jit(solution)/shard_map/ppermute | solution.py:218
  13.5 5.2 %collective-permute-start.10 = (f32[16,128]{1,0:T(8,128)S(1)}, f32[16,128]{1,0:T(8,128)S(1)}, u32[]{:S(2)}, u32[]{:S(2)}) collective-permute-start(f32[16,128]{1,0:T(8,128)S(1)} %get-tuple-element.39), channel_id=1, source_target_pairs={{0,4},{1,7},{2,6},{3,5},{4,0},{5,3},{6,2},{7,1},{8,12},{9,15},{10,... | collective-permute-start | bytes 24584 | tf_op jit(solution)/shard_map/ppermute | solution.py:215
  14.6 5.4 %collective-permute-start.11 = (f32[16,128]{1,0:T(8,128)S(1)}, f32[16,128]{1,0:T(8,128)S(1)}, u32[]{:S(2)}, u32[]{:S(2)}) collective-permute-start(f32[16,128]{1,0:T(8,128)S(1)} %get-tuple-element.40), channel_id=1, source_target_pairs={{0,12},{1,15},{2,14},{3,13},{4,8},{5,11},{6,10},{7,9},{8,4},{9,7},... | collective-permute-start | bytes 24584 | tf_op jit(solution)/shard_map/ppermute | solution.py:215
  16.9 4.5 %collective-permute-start.8 = (f32[16,128]{1,0:T(8,128)S(1)}, f32[16,128]{1,0:T(8,128)S(1)}, u32[]{:S(2)}, u32[]{:S(2)}) collective-permute-start(f32[16,128]{1,0:T(8,128)S(1)} %get-tuple-element.37), channel_id=1, source_target_pairs={{0,8},{1,11},{2,10},{3,9},{4,12},{5,15},{6,14},{7,13},{8,0},{9,3},... | collective-permute-start | bytes 24584 | tf_op jit(solution)/shard_map/ppermute | solution.py:215
  17.2 4.3 %collective-permute-start.9 = (f32[16,128]{1,0:T(8,128)S(1)}, f32[16,128]{1,0:T(8,128)S(1)}, u32[]{:S(2)}, u32[]{:S(2)}) collective-permute-start(f32[16,128]{1,0:T(8,128)S(1)} %get-tuple-element.38), channel_id=1, source_target_pairs={{0,2},{1,3},{2,0},{3,1},{4,6},{5,7},{6,4},{7,5},{8,10},{9,11},{10,... | collective-permute-start | bytes 24584 | tf_op jit(solution)/shard_map/ppermute | solution.py:215
  21.5 1.3 %collective-permute-start.12 = (f32[16,128]{1,0:T(8,128)S(1)}, f32[16,128]{1,0:T(8,128)S(1)}, u32[]{:S(2)}, u32[]{:S(2)}) collective-permute-start(f32[16,128]{1,0:T(8,128)S(1)} %shard_map.52.sums_ref), channel_id=1, source_target_pairs={{0,1},{1,0},{2,3},{3,2},{4,5},{5,4},{6,7},{7,6},{8,9},{9,8},{10,11... | collective-permute-start | bytes 24584 | tf_op jit(solution)/shard_map/ppermute | solution.py:218

commit v5 on v4

--- a/solution.py
+++ b/solution.py
@@ -17,15 +17,18 @@
     return pltpu.with_memory_space_constraint(x, pltpu.VMEM)
 
 
+NEXT = (1, 1)
+
+
 def chip_pairs(chips):
     odd = list(range(3, chips, 2))
-    return list(zip(range(chips - 2, 0, -2), odd[1:] + odd[:1])) + [(1, 1)]
+    return list(zip(range(chips - 2, 0, -2), odd[1:] + odd[:1]))
 
 
 def way_back(pairs):
-    couples = sorted((a, a + 1) for a, b in pairs if a != b)
-    first = couples.pop(len(couples) // 2) if couples else (1, 1)
-    return [first] + [(1, 1)] * bool(pairs[1:]) + couples
+    couples = sorted((a, a + 1) for a, b in pairs)
+    first = couples.pop(len(couples) // 2)
+    return [first] + couples
 
 
 def place():
@@ -63,7 +66,7 @@
     column = lax.broadcasted_iota(jnp.int32, (out_rows, rows * tiles), 1)
     slot, rest = row // (rows * per), row % (rows * per)
     target = jnp.zeros_like(row)
-    for s, pair in enumerate([(0, 0)] + pairs):
+    for s, pair in enumerate([(0, 0), NEXT] + pairs):
         target = jnp.where(slot == s, met_chip(pair), target)
     wanted = rest // per * tiles + target * per + rest % per
     choose = (column == wanted).astype(own_s.dtype)
@@ -75,10 +78,7 @@
             picked = jnp.dot(choose, flat, preferred_element_type=F32)
             for s, out in enumerate(out_refs):
                 block = picked[s * rows * per : (s + 1) * rows * per]
-                if out.shape[0] > dates:
-                    out[first * dates + d] = block.astype(out.dtype)
-                elif scenes is own_s:
-                    out[d] = block.astype(out.dtype)
+                out[first * dates + d] = block.astype(out.dtype)
 
 
 def spread(pair_rows, rows):
@@ -91,32 +91,33 @@
     )
 
 
-def dates_of(pairs, refs, counts, dates):
-    _, core = place()
-    _, rows, pixels = refs[0].shape
+def dates_of(ref, pair, counts, dates, mine=False):
+    _, core = place()
+    held, rows, pixels = ref.shape
     row = lax.broadcasted_iota(jnp.int32, (rows, pixels), 0)
-    for s, (ref, pair) in enumerate(zip(refs, [(0, 0)] + pairs)):
-        skipped = core * dates if pair[0] == pair[1] else 0
-        held = []
-        for j in range(ref.shape[0]):
-            both = ref[j].astype(F32)
-            date = met_chip(pair) * (CORES * dates) + skipped + j
-            covered = (counts > date.astype(F32)).astype(F32)
-            covered = jnp.concatenate([covered] * (pixels // LANES), axis=1)
-            weight = both[rows - CORES :] * covered
-            values = jnp.where(row < rows - CORES, both, 1.0)
-            held.append((4 * (skipped + j), values, spread(weight, rows)))
-        yield s, held
+    for j in range(dates if mine else held):
+        at = core * dates + j if mine else j
+        both = ref[at].astype(F32)
+        date = met_chip(pair) * held + at
+        covered = (counts > date.astype(F32)).astype(F32)
+        covered = jnp.concatenate([covered] * (pixels // LANES), axis=1)
+        weight = both[rows - CORES :] * covered
+        values = jnp.where(row < rows - CORES, both, 1.0)
+        yield 4 * j, values, spread(weight, rows)
+
+
+def weighted(refs, pairs, counts, dates):
+    return sum(
+        weight * values
+        for ref, pair in zip(refs, pairs)
+        for _, values, weight in dates_of(ref, pair, counts, dates)
+    )
 
 
 def partial_kernel(pairs, dates, info_ref, *refs):
     *refs, out_ref = refs
-    pixels = refs[0].shape[-1]
-    total = jnp.zeros(out_ref.shape, F32)
-    for _, held in dates_of(pairs, refs, info_ref[:, pixels:], dates):
-        for _, values, weight in held:
-            total += weight * values
-    out_ref[...] = total
+    counts = info_ref[:, refs[0].shape[-1] :]
+    out_ref[...] = weighted(refs, pairs, counts, dates)
 
 
 def columns_of(terms, rows):
@@ -128,39 +129,57 @@
     return block
 
 
-def own_sums_kernel(pairs, dates, info_ref, *refs):
-    count = len(pairs) + 1
-    refs, out_refs = refs[:count], refs[count:]
-    _, rows, pixels = refs[0].shape
+def own_sums_kernel(pairs, dates, info_ref, own_ref, *refs):
+    count = len(pairs)
+    refs, part_ref, out_refs = refs[:count], refs[count], refs[count + 1 :]
+    _, rows, pixels = own_ref.shape
+    counts = info_ref[:, pixels:]
     pif = spread(info_ref[:, :pixels], rows)
-    for s, held in dates_of(pairs, refs, info_ref[:, pixels:], dates):
+    part_ref[...] = weighted([own_ref], [(0, 0)], counts, dates)
+    blocks = [(own_ref, (0, 0), True)] + [(r, p, False) for r, p in zip(refs, pairs)]
+    for out, (ref, pair, mine) in zip(out_refs, blocks):
         terms = []
-        for k, values, weight in held:
+        for k, values, weight in dates_of(ref, pair, counts, dates, mine):
             fitted = weight * pif * values
             terms += [(k, fitted), (k + 1, fitted * values)]
-        out_refs[s][...] = columns_of(terms, rows)
-
-
-def cross_sums_kernel(pairs, dates, info_ref, part_ref, got_ref, *refs):
-    count = len(pairs) + 1
-    refs, own_refs, out_refs = refs[:count], refs[count : 2 * count], refs[2 * count :]
-    _, rows, pixels = refs[0].shape
+        out[...] = columns_of(terms, rows)
+
+
+def cross_sums_kernel(pairs, dates, info_ref, next_ref, own_ref, *refs):
+    count = len(pairs)
+    refs, (mine_ref, mate_ref, here_ref, own_sums, *sums), out_refs = (
+        refs[:count],
+        refs[count : 2 * count + 4],
+        refs[2 * count + 4 :],
+    )
+    _, rows, pixels = own_ref.shape
+    counts = info_ref[:, pixels:]
     pif = spread(info_ref[:, :pixels], rows)
-    total = part_ref[...] + got_ref[...]
+    total = mine_ref[...] + mate_ref[...] + here_ref[...]
+    total += weighted([next_ref], [NEXT], counts, dates)
     composite = total / spread(total[rows - CORES :], rows)
-    blocks = []
-    for s, held in dates_of(pairs, refs, info_ref[:, pixels:], dates):
+
+    def block(ref, pair, mine, add):
         terms = []
-        for k, values, weight in held:
+        for k, values, weight in dates_of(ref, pair, counts, dates, mine):
             fit = weight * pif * composite
             terms += [(k + 2, fit), (k + 3, fit * values)]
-        blocks.append(own_refs[s][...] + columns_of(terms, rows))
-    _, core = place()
-    out_refs[0][...] = blocks[0]
+        return columns_of(terms, rows) + add[...]
+
+    for k, values, weight in dates_of(next_ref, NEXT, counts, dates, True):
+        fit = weight * pif
+        cross = fit * composite
+        terms = (fit * values, fit * values * values, cross, cross * values)
+        terms = [(k + extra, term) for extra, term in enumerate(terms)]
+        out_refs[1][k // 4] = columns_of(terms, rows)
+    out_refs[0][...] = block(own_ref, (0, 0), True, own_sums)
+    blocks = [block(r, p, False, add) for r, p, add in zip(refs, pairs, sums)]
+    _, core = place()
     near_by, far_off = zip(*pairs)
-    for out, (a, b) in zip(out_refs[1:], way_back(pairs)):
-        first, second = near_by.index(a) + 1, far_off.index(b) + 1
-        out[...] = jnp.where(core == 0, blocks[first], blocks[second])
+    for out, (a, b) in zip(out_refs[2:], way_back(pairs)):
+        out[...] = jnp.where(
+            core == 0, blocks[near_by.index(a)], blocks[far_off.index(b)]
+        )
 
 
 def sum_kernel(*refs):
@@ -168,10 +187,16 @@
     out_ref[...] = sum(ref[...] for ref in refs)
 
 
+def join_kernel(dates, own_ref, mine_ref, mate_ref, out_ref):
+    _, core = place()
+    sums = mine_ref[...] + mate_ref[...]
+    sums = jnp.where(core == 0, sums, pltpu.roll(sums, LANES - 4 * dates, 1))
+    out_ref[...] = own_ref[...] + sums
+
+
 def apply_kernel(sums_ref, got_ref, scenes_ref, out_ref, done_ref, sems):
     dates, bands, tiles, pixels = scenes_ref.shape
-    _, core = place()
-    sums = sums_ref[...] + got_ref[...]
+    sums = sums_ref[...] + jnp.sum(got_ref[...], axis=0)
     sum_x = sums + pltpu.roll(sums, sums.shape[0] - 1, 0)
     sum_xx, sum_y, sum_xy = (pltpu.roll(sum_x, LANES - k, 1) for k in (1, 2, 3))
     last = CORES * bands
@@ -185,12 +210,7 @@
     for d in range(dates):
         shape = (sums.shape[0], pixels)
         slope, shift = (
-            jnp.where(
-                core == 0,
-                jnp.broadcast_to(x[:, 4 * d : 4 * d + 1], shape),
-                jnp.broadcast_to(x[:, 4 * (d + dates) : 4 * (d + dates) + 1], shape),
-            )
-            for x in (gain, offset)
+            jnp.broadcast_to(x[:, 4 * d : 4 * d + 1], shape) for x in (gain, offset)
         )
         for b in range(bands):
             r = CORES * b
@@ -237,13 +257,10 @@
         quality,
         pif_mask,
     )
-    blocks = [
-        pltpu.VMEM((dates * (1 if a == b else CORES), rows, pixels), scenes.dtype)
-        for a, b in [(0, 0)] + pairs
-    ]
-    own, *sent = call(
+    block = pltpu.VMEM((CORES * dates, rows, pixels), scenes.dtype)
+    own, beside, *sent = call(
         functools.partial(pack_kernel, pairs),
-        blocks,
+        [block] * (len(pairs) + 2),
         own_scenes,
         own_quality,
         mate_scenes,
@@ -257,28 +274,36 @@
         in_specs=[VMEM, SMEM],
     )
     info = info + mate(info)
-    held = [own] + [swap(x, pair) for x, pair in zip(sent, pairs)]
-    part = call(
-        functools.partial(partial_kernel, pairs, dates),
-        pltpu.VMEM((rows, pixels), F32),
+    held = [swap(x, pair) for x, pair in zip(sent, pairs)]
+    beside = swap(beside, NEXT)
+    wide = pltpu.VMEM((rows, pixels), F32)
+    sums = pltpu.VMEM((rows, LANES), F32)
+    part = call(functools.partial(partial_kernel, pairs, dates), wide, info, *held)
+    here, *own_sums = call(
+        functools.partial(own_sums_kernel, pairs, dates),
+        [wide] + [sums] * (len(pairs) + 1),
         info,
+        own,
         *held,
     )
-    sums = [pltpu.VMEM((rows, LANES), F32)] * len(held)
-    own_sums = call(
-        functools.partial(own_sums_kernel, pairs, dates), sums, info, *held
-    )
-    own, *sent = call(
+    own, beside, *sent = call(
         functools.partial(cross_sums_kernel, pairs, dates),
-        sums,
+        [sums, pltpu.VMEM((dates, rows, LANES), F32)] + [sums] * len(pairs),
         info,
+        beside,
+        own,
+        *held,
         part,
         mate(part),
-        *held,
+        here,
         *own_sums,
     )
     back = [swap(x, pair) for x, pair in zip(sent, way_back(pairs))]
-    total = call(sum_kernel, sums[0], own, *back)
+    beside = swap(beside, NEXT)
+    back = call(sum_kernel, sums, *back)
+    total = call(
+        functools.partial(join_kernel, dates), sums, own, back, mate(back)
+    )
     out = pl.pallas_call(
         apply_kernel,
         out_shape=jax.ShapeDtypeStruct(scenes.shape, scenes.dtype),
@@ -288,7 +313,7 @@
             pltpu.VMEM(scenes.shape, scenes.dtype),
             pltpu.SemaphoreType.DMA((dates,)),
         ],
-    )(near(total), near(mate(total)), near(own_scenes))
+    )(near(total), near(beside), near(own_scenes))
     return out.transpose(0, 2, 1, 3)
 
 

time: 23.8 us -> 23.1 us (0.971)
  waiting for transfers between devices: 6.54 us -> 5.53 us
    ppermute x8, waiting for transfers between devices: 3.66 us -> 2.32 us  [swap(): lax.ppermute(x, 'dates', [(i, i ^ hop[i % CORES]) for i in range(size)])]
    ppermute x8, starting transfers between devices: 12.3 us -> 13 us  [swap(): lax.ppermute(x, 'dates', [(i, i ^ hop[i % CORES]) for i in range(size)])]
    ppermute x5, starting transfers between devices: 1.73 us -> 1.23 us  [mate(): return lax.ppermute(x, 'dates', [(i, i ^ 1) for i in range(size)])]
    ppermute x5, waiting for transfers between devices: 2.88 us -> 3.2 us  [mate(): return lax.ppermute(x, 'dates', [(i, i ^ 1) for i in range(size)])]
    pallas_call x7 -> x8, Pallas kernels: 1.55 us -> 1.64 us  [call(): pl.pallas_call(kernel, out_shape=out_shape, in_specs=in_specs or [VMEM] *...]
  transfers between devices with their start and end apart: 13 -> 13, of which waited for: 8 -> 6; matrix products, arithmetic and copies ran while one was open for 0% -> 0% of each run, Pallas kernels for 5% -> 5%
where the time goes in v5:
time: 23.1 us; the launch traced here: 23 us
  starting transfers between devices  14.2 us (61%)
  waiting for transfers between devices  5.53 us (24%)
  Pallas kernels  2.48 us (11%)
  between operations  0.71 us (3%)
    ppermute x8, starting transfers between devices, swap(): lax.ppermute(x, 'dates', [(i, i ^ hop[i % CORES]) for i in range(size)])  13 us
    ppermute x5, waiting for transfers between devices, mate(): return lax.ppermute(x, 'dates', [(i, i ^ 1) for i in range(size)])  3.2 us
    ppermute x8, waiting for transfers between devices, swap(): lax.ppermute(x, 'dates', [(i, i ^ hop[i % CORES]) for i in range(size)])  2.32 us
    pallas_call x8, Pallas kernels, call(): pl.pallas_call(kernel, out_shape=out_shape, in_specs=in_specs or [VMEM] *...  1.64 us
    ppermute x5, starting transfers between devices, mate(): return lax.ppermute(x, 'dates', [(i, i ^ 1) for i in range(size)])  1.23 us
    pallas_call x1, Pallas kernels, local(): pl.pallas_call(apply_kernel, out_shape=jax.ShapeDtypeStruct(scenes.shape,...  0.84 us
  transfers between devices with their start and end apart: 13, of which 6 were waited for; matrix products, arithmetic and copies ran while one was open for 0% of the time, Pallas kernels for 5%

profile of v5, /device:TPU:0, one launch (start us, length us, event | category | flops | bytes accessed | tf_op | source)
XLA Modules:
  0.0 23.0 jit_solution(3735493354603935199)
XLA Ops:
  0.0 0.5 %collective-permute-start.1 = (bf16[2,7,16,256]{3,2,1,0:T(8,128)(2,1)}, bf16[2,7,16,256]{3,2,1,0:T(8,128)(2,1)S(1)}, u32[]{:S(2)}, u32[]{:S(2)}) collective-permute-start(bf16[2,7,16,256]{3,2,1,0:T(8,128)(2,1)} %bitcast.2), channel_id=1, source_target_pairs={{0,1},{1,0},{2,3},{3,2},{4,5},{5,4},{6,7},{7,6},{8,9},{9,8},{10,11... | collective-permute-start | bytes 344072 | tf_op jit(solution)/shard_map/ppermute | solution.py:238
  0.5 0.1 collective-permute-start.2
  0.5 0.9 %shard_map.46 = (bf16[2,7,16,256]{3,2,1,0:T(8,128)(2,1)S(1)}, bf16[2,16,256]{2,1,0:T(8,128)(2,1)S(1)}, f32[1,256]{1,0:T(1,128)S(1)}) custom-call(bf16[2,7,16,256]{3,2,1,0:T(8,128)(2,1)} %bitcast.3, bf16[2,16,256]{2,1,0:T(8,128)(2,1)} %refs_1_.1, f32[1,256]{1,0:T(1,128)} %refs_2_.1), custom_call_target="tpu_custom_call" | custom-call | tf_op jit(solution)/shard_map/pallas_call | solution.py:245
  1.4 0.4 %collective-permute-done.2.mate_q = bf16[2,16,256]{2,1,0:T(8,128)(2,1)S(1)} collective-permute-done((bf16[2,16,256]{2,1,0:T(8,128)(2,1)}, bf16[2,16,256]{2,1,0:T(8,128)(2,1)S(1)}, u32[]{:S(2)}, u32[]{:S(2)}) %collective-permute-start.2) | collective-permute-done | bytes 16416 | tf_op jit(solution)/shard_map/ppermute | solution.py:238
  1.8 0.0 collective-permute-done.1.mate_s
  1.9 0.2 shard_map.48
  2.0 4.8 %collective-permute-start.4 = (bf16[4,16,256]{2,1,0:T(8,128)(2,1)S(1)}, bf16[4,16,256]{2,1,0:T(8,128)(2,1)S(1)}, u32[]{:S(2)}, u32[]{:S(2)}) collective-permute-start(bf16[4,16,256]{2,1,0:T(8,128)(2,1)S(1)} %get-tuple-element.28), channel_id=1, source_target_pairs={{0,12},{1,11},{2,14},{3,9},{4,8},{5,15},{6,10},{7,13},{8,4},{9,3},... | collective-permute-start | bytes 98312 | tf_op jit(solution)/shard_map/ppermute | solution.py:235
  6.9 0.0 collective-permute-start.5
  6.9 0.6 %collective-permute-start.6 = (bf16[4,16,256]{2,1,0:T(8,128)(2,1)S(1)}, bf16[4,16,256]{2,1,0:T(8,128)(2,1)S(1)}, u32[]{:S(2)}, u32[]{:S(2)}) collective-permute-start(bf16[4,16,256]{2,1,0:T(8,128)(2,1)S(1)} %get-tuple-element.30), channel_id=1, source_target_pairs={{0,4},{1,7},{2,6},{3,5},{4,0},{5,3},{6,2},{7,1},{8,12},{9,15},{10,... | collective-permute-start | bytes 98312 | tf_op jit(solution)/shard_map/ppermute | solution.py:235
  7.5 1.7 %collective-permute-start.3 = (bf16[4,16,256]{2,1,0:T(8,128)(2,1)S(1)}, bf16[4,16,256]{2,1,0:T(8,128)(2,1)S(1)}, u32[]{:S(2)}, u32[]{:S(2)}) collective-permute-start(bf16[4,16,256]{2,1,0:T(8,128)(2,1)S(1)} %get-tuple-element.26), channel_id=1, source_target_pairs={{0,2},{1,3},{2,0},{3,1},{4,6},{5,7},{6,4},{7,5},{8,10},{9,11},{10,... | collective-permute-start | bytes 98312 | tf_op jit(solution)/shard_map/ppermute | solution.py:235
  9.8 0.2 %collective-permute-start = (f32[2,384]{1,0:T(2,128)S(1)}, f32[2,384]{1,0:T(2,128)S(1)}, u32[]{:S(2)}, u32[]{:S(2)}) collective-permute-start(f32[2,384]{1,0:T(2,128)S(1)} %shard_map.47), channel_id=1, source_target_pairs={{0,1},{1,0},{2,3},{3,2},{4,5},{5,4},{6,7},{7,6},{8,9},{9,8},{10,11... | collective-permute-start | bytes 9224 | tf_op jit(solution)/shard_map/ppermute | solution.py:238
  10.1 1.0 %collective-permute-done = f32[2,384]{1,0:T(2,128)S(1)} collective-permute-done((f32[2,384]{1,0:T(2,128)S(1)}, f32[2,384]{1,0:T(2,128)S(1)}, u32[]{:S(2)}, u32[]{:S(2)}) %collective-permute-start) | collective-permute-done | bytes 3104 | tf_op jit(solution)/shard_map/ppermute | solution.py:238
  11.1 0.0 collective-permute-done.4.refs_0_
  11.1 0.9 %collective-permute-done.5.refs_1_ = bf16[4,16,256]{2,1,0:T(8,128)(2,1)S(1)} collective-permute-done((bf16[4,16,256]{2,1,0:T(8,128)(2,1)S(1)}, bf16[4,16,256]{2,1,0:T(8,128)(2,1)S(1)}, u32[]{:S(2)}, u32[]{:S(2)}) %collective-permute-start.5) | collective-permute-done | bytes 32800 | tf_op jit(solution)/shard_map/ppermute | solution.py:235
  12.0 0.0 collective-permute-done.6.refs_2_
  12.0 0.1 shard_map.49.refs_3_
  12.0 0.5 %collective-permute-start.7 = (f32[16,256]{1,0:T(8,128)S(1)}, f32[16,256]{1,0:T(8,128)S(1)}, u32[]{:S(2)}, u32[]{:S(2)}) collective-permute-start(f32[16,256]{1,0:T(8,128)S(1)} %shard_map.49.refs_3_), channel_id=1, source_target_pairs={{0,1},{1,0},{2,3},{3,2},{4,5},{5,4},{6,7},{7,6},{8,9},{9,8},{10,11... | collective-permute-start | bytes 49160 | tf_op jit(solution)/shard_map/ppermute | solution.py:238
  12.5 0.2 shard_map.50
  12.7 0.0 collective-permute-done.3.next_ref
  12.7 0.6 %collective-permute-done.7.refs_4_ = f32[16,256]{1,0:T(8,128)S(1)} collective-permute-done((f32[16,256]{1,0:T(8,128)S(1)}, f32[16,256]{1,0:T(8,128)S(1)}, u32[]{:S(2)}, u32[]{:S(2)}) %collective-permute-start.7) | collective-permute-done | bytes 16416 | tf_op jit(solution)/shard_map/ppermute | solution.py:238
  13.3 0.2 shard_map.51
  13.5 2.8 %collective-permute-start.10 = (f32[16,128]{1,0:T(8,128)S(1)}, f32[16,128]{1,0:T(8,128)S(1)}, u32[]{:S(2)}, u32[]{:S(2)}) collective-permute-start(f32[16,128]{1,0:T(8,128)S(1)} %get-tuple-element.39), channel_id=1, source_target_pairs={{0,12},{1,15},{2,14},{3,13},{4,8},{5,11},{6,10},{7,9},{8,4},{9,7},... | collective-permute-start | bytes 24584 | tf_op jit(solution)/shard_map/ppermute | solution.py:235
  16.3 0.0 collective-permute-start.8
  16.3 1.7 %collective-permute-start.9 = (f32[16,128]{1,0:T(8,128)S(1)}, f32[16,128]{1,0:T(8,128)S(1)}, u32[]{:S(2)}, u32[]{:S(2)}) collective-permute-start(f32[16,128]{1,0:T(8,128)S(1)} %get-tuple-element.38), channel_id=1, source_target_pairs={{0,4},{1,7},{2,6},{3,5},{4,0},{5,3},{6,2},{7,1},{8,12},{9,15},{10,... | collective-permute-start | bytes 24584 | tf_op jit(solution)/shard_map/ppermute | solution.py:235
  18.0 1.4 %collective-permute-start.12 = (f32[2,16,128]{2,1,0:T(8,128)S(1)}, f32[2,16,128]{2,1,0:T(8,128)S(1)}, u32[]{:S(2)}, u32[]{:S(2)}) collective-permute-start(f32[2,16,128]{2,1,0:T(8,128)S(1)} %get-tuple-element.40), channel_id=1, source_target_pairs={{0,2},{1,3},{2,0},{3,1},{4,6},{5,7},{6,4},{7,5},{8,10},{9,11},{10,... | collective-permute-start | bytes 49160 | tf_op jit(solution)/shard_map/ppermute | solution.py:235
  19.4 0.0 collective-permute-done.10.refs_2_
  19.4 1.4 %collective-permute-done.8.refs_0_ = f32[16,128]{1,0:T(8,128)S(1)} collective-permute-done((f32[16,128]{1,0:T(8,128)S(1)}, f32[16,128]{1,0:T(8,128)S(1)}, u32[]{:S(2)}, u32[]{:S(2)}) %collective-permute-start.8) | collective-permute-done | bytes 8224 | tf_op jit(solution)/shard_map/ppermute | solution.py:235
  20.8 0.0 collective-permute-done.9.refs_1_
  20.9 0.0 collective-permute-start.11
  20.9 1.2 %collective-permute-done.11.mate_ref = f32[16,128]{1,0:T(8,128)S(1)} collective-permute-done((f32[16,128]{1,0:T(8,128)S(1)}, f32[16,128]{1,0:T(8,128)S(1)}, u32[]{:S(2)}, u32[]{:S(2)}) %collective-permute-start.11) | collective-permute-done | bytes 8224 | tf_op jit(solution)/shard_map/ppermute | solution.py:238
  22.0 0.1 shard_map.53.sums_ref
  22.1 0.0 collective-permute-done.12.got_ref
  22.1 0.8 %shard_map.54 = bf16[2,7,16,256]{3,2,1,0:T(8,128)(2,1)} custom-call(f32[16,128]{1,0:T(8,128)S(1)} %shard_map.53.sums_ref, f32[2,16,128]{2,1,0:T(8,128)S(1)} %collective-permute-done.12.got_ref, bf16[2,7,16,256]{3,2,1,0:T(8,128)(2,1)S(1)} %get-tuple-element.24.own_s.scenes_ref), custom_call_target="tpu_custom_call" | custom-call | tf_op jit(solution)/shard_map/pallas_call | solution.py:307
  (3 shorter events, 0.0 us)
Async XLA Ops:
  0.0 1.9 %collective-permute-start.1 = (bf16[2,7,16,256]{3,2,1,0:T(8,128)(2,1)}, bf16[2,7,16,256]{3,2,1,0:T(8,128)(2,1)S(1)}, u32[]{:S(2)}, u32[]{:S(2)}) collective-permute-start(bf16[2,7,16,256]{3,2,1,0:T(8,128)(2,1)} %bitcast.2), channel_id=1, source_target_pairs={{0,1},{1,0},{2,3},{3,2},{4,5},{5,4},{6,7},{7,6},{8,9},{9,8},{10,11... | collective-permute-start | bytes 344072 | tf_op jit(solution)/shard_map/ppermute | solution.py:238
  0.5 1.4 %collective-permute-start.2 = (bf16[2,16,256]{2,1,0:T(8,128)(2,1)}, bf16[2,16,256]{2,1,0:T(8,128)(2,1)S(1)}, u32[]{:S(2)}, u32[]{:S(2)}) collective-permute-start(bf16[2,16,256]{2,1,0:T(8,128)(2,1)} %refs_1_.1), channel_id=1, source_target_pairs={{0,1},{1,0},{2,3},{3,2},{4,5},{5,4},{6,7},{7,6},{8,9},{9,8},{10,11... | collective-permute-start | bytes 49160 | tf_op jit(solution)/shard_map/ppermute | solution.py:238
  2.0 9.0 %collective-permute-start.4 = (bf16[4,16,256]{2,1,0:T(8,128)(2,1)S(1)}, bf16[4,16,256]{2,1,0:T(8,128)(2,1)S(1)}, u32[]{:S(2)}, u32[]{:S(2)}) collective-permute-start(bf16[4,16,256]{2,1,0:T(8,128)(2,1)S(1)} %get-tuple-element.28), channel_id=1, source_target_pairs={{0,12},{1,11},{2,14},{3,9},{4,8},{5,15},{6,10},{7,13},{8,4},{9,3},... | collective-permute-start | bytes 98312 | tf_op jit(solution)/shard_map/ppermute | solution.py:235
  6.9 5.1 %collective-permute-start.5 = (bf16[4,16,256]{2,1,0:T(8,128)(2,1)S(1)}, bf16[4,16,256]{2,1,0:T(8,128)(2,1)S(1)}, u32[]{:S(2)}, u32[]{:S(2)}) collective-permute-start(bf16[4,16,256]{2,1,0:T(8,128)(2,1)S(1)} %get-tuple-element.29), channel_id=1, source_target_pairs={{0,8},{1,15},{2,10},{3,13},{4,12},{5,11},{6,14},{7,9},{8,0},{9,7},... | collective-permute-start | bytes 98312 | tf_op jit(solution)/shard_map/ppermute | solution.py:235
  6.9 5.1 %collective-permute-start.6 = (bf16[4,16,256]{2,1,0:T(8,128)(2,1)S(1)}, bf16[4,16,256]{2,1,0:T(8,128)(2,1)S(1)}, u32[]{:S(2)}, u32[]{:S(2)}) collective-permute-start(bf16[4,16,256]{2,1,0:T(8,128)(2,1)S(1)} %get-tuple-element.30), channel_id=1, source_target_pairs={{0,4},{1,7},{2,6},{3,5},{4,0},{5,3},{6,2},{7,1},{8,12},{9,15},{10,... | collective-permute-start | bytes 98312 | tf_op jit(solution)/shard_map/ppermute | solution.py:235
  7.5 5.2 %collective-permute-start.3 = (bf16[4,16,256]{2,1,0:T(8,128)(2,1)S(1)}, bf16[4,16,256]{2,1,0:T(8,128)(2,1)S(1)}, u32[]{:S(2)}, u32[]{:S(2)}) collective-permute-start(bf16[4,16,256]{2,1,0:T(8,128)(2,1)S(1)} %get-tuple-element.26), channel_id=1, source_target_pairs={{0,2},{1,3},{2,0},{3,1},{4,6},{5,7},{6,4},{7,5},{8,10},{9,11},{10,... | collective-permute-start | bytes 98312 | tf_op jit(solution)/shard_map/ppermute | solution.py:235
  9.8 1.2 %collective-permute-start = (f32[2,384]{1,0:T(2,128)S(1)}, f32[2,384]{1,0:T(2,128)S(1)}, u32[]{:S(2)}, u32[]{:S(2)}) collective-permute-start(f32[2,384]{1,0:T(2,128)S(1)} %shard_map.47), channel_id=1, source_target_pairs={{0,1},{1,0},{2,3},{3,2},{4,5},{5,4},{6,7},{7,6},{8,9},{9,8},{10,11... | collective-permute-start | bytes 9224 | tf_op jit(solution)/shard_map/ppermute | solution.py:238
  12.0 1.3 %collective-permute-start.7 = (f32[16,256]{1,0:T(8,128)S(1)}, f32[16,256]{1,0:T(8,128)S(1)}, u32[]{:S(2)}, u32[]{:S(2)}) collective-permute-start(f32[16,256]{1,0:T(8,128)S(1)} %shard_map.49.refs_3_), channel_id=1, source_target_pairs={{0,1},{1,0},{2,3},{3,2},{4,5},{5,4},{6,7},{7,6},{8,9},{9,8},{10,11... | collective-permute-start | bytes 49160 | tf_op jit(solution)/shard_map/ppermute | solution.py:238
  13.5 5.9 %collective-permute-start.10 = (f32[16,128]{1,0:T(8,128)S(1)}, f32[16,128]{1,0:T(8,128)S(1)}, u32[]{:S(2)}, u32[]{:S(2)}) collective-permute-start(f32[16,128]{1,0:T(8,128)S(1)} %get-tuple-element.39), channel_id=1, source_target_pairs={{0,12},{1,15},{2,14},{3,13},{4,8},{5,11},{6,10},{7,9},{8,4},{9,7},... | collective-permute-start | bytes 24584 | tf_op jit(solution)/shard_map/ppermute | solution.py:235
  16.3 4.5 %collective-permute-start.8 = (f32[16,128]{1,0:T(8,128)S(1)}, f32[16,128]{1,0:T(8,128)S(1)}, u32[]{:S(2)}, u32[]{:S(2)}) collective-permute-start(f32[16,128]{1,0:T(8,128)S(1)} %get-tuple-element.37), channel_id=1, source_target_pairs={{0,8},{1,11},{2,10},{3,9},{4,12},{5,15},{6,14},{7,13},{8,0},{9,3},... | collective-permute-start | bytes 24584 | tf_op jit(solution)/shard_map/ppermute | solution.py:235
  16.3 4.5 %collective-permute-start.9 = (f32[16,128]{1,0:T(8,128)S(1)}, f32[16,128]{1,0:T(8,128)S(1)}, u32[]{:S(2)}, u32[]{:S(2)}) collective-permute-start(f32[16,128]{1,0:T(8,128)S(1)} %get-tuple-element.38), channel_id=1, source_target_pairs={{0,4},{1,7},{2,6},{3,5},{4,0},{5,3},{6,2},{7,1},{8,12},{9,15},{10,... | collective-permute-start | bytes 24584 | tf_op jit(solution)/shard_map/ppermute | solution.py:235
  18.0 4.1 %collective-permute-start.12 = (f32[2,16,128]{2,1,0:T(8,128)S(1)}, f32[2,16,128]{2,1,0:T(8,128)S(1)}, u32[]{:S(2)}, u32[]{:S(2)}) collective-permute-start(f32[2,16,128]{2,1,0:T(8,128)S(1)} %get-tuple-element.40), channel_id=1, source_target_pairs={{0,2},{1,3},{2,0},{3,1},{4,6},{5,7},{6,4},{7,5},{8,10},{9,11},{10,... | collective-permute-start | bytes 49160 | tf_op jit(solution)/shard_map/ppermute | solution.py:235
  20.9 1.2 %collective-permute-start.11 = (f32[16,128]{1,0:T(8,128)S(1)}, f32[16,128]{1,0:T(8,128)S(1)}, u32[]{:S(2)}, u32[]{:S(2)}) collective-permute-start(f32[16,128]{1,0:T(8,128)S(1)} %shard_map.52.mine_ref), channel_id=1, source_target_pairs={{0,1},{1,0},{2,3},{3,2},{4,5},{5,4},{6,7},{7,6},{8,9},{9,8},{10,11... | collective-permute-start | bytes 24584 | tf_op jit(solution)/shard_map/ppermute | solution.py:238

commit v6 on v5

--- a/solution.py
+++ b/solution.py
@@ -26,9 +26,7 @@
 
 
 def way_back(pairs):
-    couples = sorted((a, a + 1) for a, b in pairs)
-    first = couples.pop(len(couples) // 2)
-    return [first] + couples
+    return sorted(((a, a + 1) for a, b in pairs), reverse=True)
 
 
 def place():
@@ -129,13 +127,18 @@
     return block
 
 
-def own_sums_kernel(pairs, dates, info_ref, own_ref, *refs):
+def own_sums_kernel(pairs, dates, info_ref, next_ref, own_ref, *refs):
     count = len(pairs)
     refs, part_ref, out_refs = refs[:count], refs[count], refs[count + 1 :]
     _, rows, pixels = own_ref.shape
     counts = info_ref[:, pixels:]
     pif = spread(info_ref[:, :pixels], rows)
-    part_ref[...] = weighted([own_ref], [(0, 0)], counts, dates)
+    part_ref[...] = weighted([own_ref, next_ref], [(0, 0), NEXT], counts, dates)
+    *out_refs, next_out = out_refs
+    for k, values, weight in dates_of(next_ref, NEXT, counts, dates, True):
+        fitted = weight * pif * values
+        terms = [(k, fitted), (k + 1, fitted * values)]
+        next_out[k // 4] = columns_of(terms, rows)
     blocks = [(own_ref, (0, 0), True)] + [(r, p, False) for r, p in zip(refs, pairs)]
     for out, (ref, pair, mine) in zip(out_refs, blocks):
         terms = []
@@ -147,16 +150,15 @@
 
 def cross_sums_kernel(pairs, dates, info_ref, next_ref, own_ref, *refs):
     count = len(pairs)
-    refs, (mine_ref, mate_ref, here_ref, own_sums, *sums), out_refs = (
+    refs, (mine_ref, mate_ref, here_ref, own_sums, *sums, next_sums), out_refs = (
         refs[:count],
-        refs[count : 2 * count + 4],
-        refs[2 * count + 4 :],
+        refs[count : 2 * count + 5],
+        refs[2 * count + 5 :],
     )
     _, rows, pixels = own_ref.shape
     counts = info_ref[:, pixels:]
     pif = spread(info_ref[:, :pixels], rows)
     total = mine_ref[...] + mate_ref[...] + here_ref[...]
-    total += weighted([next_ref], [NEXT], counts, dates)
     composite = total / spread(total[rows - CORES :], rows)
 
     def block(ref, pair, mine, add):
@@ -167,11 +169,9 @@
         return columns_of(terms, rows) + add[...]
 
     for k, values, weight in dates_of(next_ref, NEXT, counts, dates, True):
-        fit = weight * pif
-        cross = fit * composite
-        terms = (fit * values, fit * values * values, cross, cross * values)
-        terms = [(k + extra, term) for extra, term in enumerate(terms)]
-        out_refs[1][k // 4] = columns_of(terms, rows)
+        fit = weight * pif * composite
+        terms = [(k + 2, fit), (k + 3, fit * values)]
+        out_refs[1][k // 4] = next_sums[k // 4] + columns_of(terms, rows)
     out_refs[0][...] = block(own_ref, (0, 0), True, own_sums)
     blocks = [block(r, p, False, add) for r, p, add in zip(refs, pairs, sums)]
     _, core = place()
@@ -281,8 +281,9 @@
     part = call(functools.partial(partial_kernel, pairs, dates), wide, info, *held)
     here, *own_sums = call(
         functools.partial(own_sums_kernel, pairs, dates),
-        [wide] + [sums] * (len(pairs) + 1),
+        [wide] + [sums] * (len(pairs) + 1) + [pltpu.VMEM((dates, rows, LANES), F32)],
         info,
+        beside,
         own,
         *held,
     )

time: 23.1 us -> 23.1 us (level)
  transfers between devices with their start and end apart: 13 -> 13, of which waited for: 6 -> 6; matrix products, arithmetic and copies ran while one was open for 0% -> 0% of each run, Pallas kernels for 5% -> 6%
where the time goes in v6:
time: 23.1 us; the launch traced here: 22.9 us
  starting transfers between devices  14.2 us (61%)
  waiting for transfers between devices  5.51 us (24%)
  Pallas kernels  2.49 us (11%)
  between operations  0.7 us (3%)
    ppermute x8, starting transfers between devices, swap(): lax.ppermute(x, 'dates', [(i, i ^ hop[i % CORES]) for i in range(size)])  13 us
    ppermute x5, waiting for transfers between devices, mate(): return lax.ppermute(x, 'dates', [(i, i ^ 1) for i in range(size)])  3.19 us
    ppermute x8, waiting for transfers between devices, swap(): lax.ppermute(x, 'dates', [(i, i ^ hop[i % CORES]) for i in range(size)])  2.32 us
    pallas_call x8, Pallas kernels, call(): pl.pallas_call(kernel, out_shape=out_shape, in_specs=in_specs or [VMEM] *...  1.64 us
    ppermute x5, starting transfers between devices, mate(): return lax.ppermute(x, 'dates', [(i, i ^ 1) for i in range(size)])  1.23 us
    pallas_call x1, Pallas kernels, local(): pl.pallas_call(apply_kernel, out_shape=jax.ShapeDtypeStruct(scenes.shape,...  0.84 us
  transfers between devices with their start and end apart: 13, of which 6 were waited for; matrix products, arithmetic and copies ran while one was open for 0% of the time, Pallas kernels for 6%

profile of v6, /device:TPU:0, one launch (start us, length us, event | category | flops | bytes accessed | tf_op | source)
XLA Modules:
  0.0 22.9 jit_solution(7729294965062314230)
XLA Ops:
  0.0 0.5 %collective-permute-start.1 = (bf16[2,7,16,256]{3,2,1,0:T(8,128)(2,1)}, bf16[2,7,16,256]{3,2,1,0:T(8,128)(2,1)S(1)}, u32[]{:S(2)}, u32[]{:S(2)}) collective-permute-start(bf16[2,7,16,256]{3,2,1,0:T(8,128)(2,1)} %bitcast.2), channel_id=1, source_target_pairs={{0,1},{1,0},{2,3},{3,2},{4,5},{5,4},{6,7},{7,6},{8,9},{9,8},{10,11... | collective-permute-start | bytes 344072 | tf_op jit(solution)/shard_map/ppermute | solution.py:238
  0.5 0.1 collective-permute-start.2
  0.5 0.9 %shard_map.46 = (bf16[2,7,16,256]{3,2,1,0:T(8,128)(2,1)S(1)}, bf16[2,16,256]{2,1,0:T(8,128)(2,1)S(1)}, f32[1,256]{1,0:T(1,128)S(1)}) custom-call(bf16[2,7,16,256]{3,2,1,0:T(8,128)(2,1)} %bitcast.3, bf16[2,16,256]{2,1,0:T(8,128)(2,1)} %refs_1_.1, f32[1,256]{1,0:T(1,128)} %refs_2_.1), custom_call_target="tpu_custom_call" | custom-call | tf_op jit(solution)/shard_map/pallas_call | solution.py:245
  1.4 0.4 %collective-permute-done.2.mate_q = bf16[2,16,256]{2,1,0:T(8,128)(2,1)S(1)} collective-permute-done((bf16[2,16,256]{2,1,0:T(8,128)(2,1)}, bf16[2,16,256]{2,1,0:T(8,128)(2,1)S(1)}, u32[]{:S(2)}, u32[]{:S(2)}) %collective-permute-start.2) | collective-permute-done | bytes 16416 | tf_op jit(solution)/shard_map/ppermute | solution.py:238
  1.8 0.0 collective-permute-done.1.mate_s
  1.9 0.2 shard_map.48
  2.0 4.8 %collective-permute-start.4 = (bf16[4,16,256]{2,1,0:T(8,128)(2,1)S(1)}, bf16[4,16,256]{2,1,0:T(8,128)(2,1)S(1)}, u32[]{:S(2)}, u32[]{:S(2)}) collective-permute-start(bf16[4,16,256]{2,1,0:T(8,128)(2,1)S(1)} %get-tuple-element.29), channel_id=1, source_target_pairs={{0,12},{1,11},{2,14},{3,9},{4,8},{5,15},{6,10},{7,13},{8,4},{9,3},... | collective-permute-start | bytes 98312 | tf_op jit(solution)/shard_map/ppermute | solution.py:235
  6.9 0.0 collective-permute-start.5
  6.9 0.6 %collective-permute-start.6 = (bf16[4,16,256]{2,1,0:T(8,128)(2,1)S(1)}, bf16[4,16,256]{2,1,0:T(8,128)(2,1)S(1)}, u32[]{:S(2)}, u32[]{:S(2)}) collective-permute-start(bf16[4,16,256]{2,1,0:T(8,128)(2,1)S(1)} %get-tuple-element.31), channel_id=1, source_target_pairs={{0,4},{1,7},{2,6},{3,5},{4,0},{5,3},{6,2},{7,1},{8,12},{9,15},{10,... | collective-permute-start | bytes 98312 | tf_op jit(solution)/shard_map/ppermute | solution.py:235
  7.5 1.7 %collective-permute-start.3 = (bf16[4,16,256]{2,1,0:T(8,128)(2,1)S(1)}, bf16[4,16,256]{2,1,0:T(8,128)(2,1)S(1)}, u32[]{:S(2)}, u32[]{:S(2)}) collective-permute-start(bf16[4,16,256]{2,1,0:T(8,128)(2,1)S(1)} %get-tuple-element.27), channel_id=1, source_target_pairs={{0,2},{1,3},{2,0},{3,1},{4,6},{5,7},{6,4},{7,5},{8,10},{9,11},{10,... | collective-permute-start | bytes 98312 | tf_op jit(solution)/shard_map/ppermute | solution.py:235
  9.8 0.2 %collective-permute-start = (f32[2,384]{1,0:T(2,128)S(1)}, f32[2,384]{1,0:T(2,128)S(1)}, u32[]{:S(2)}, u32[]{:S(2)}) collective-permute-start(f32[2,384]{1,0:T(2,128)S(1)} %shard_map.47), channel_id=1, source_target_pairs={{0,1},{1,0},{2,3},{3,2},{4,5},{5,4},{6,7},{7,6},{8,9},{9,8},{10,11... | collective-permute-start | bytes 9224 | tf_op jit(solution)/shard_map/ppermute | solution.py:238
  10.1 1.0 %collective-permute-done = f32[2,384]{1,0:T(2,128)S(1)} collective-permute-done((f32[2,384]{1,0:T(2,128)S(1)}, f32[2,384]{1,0:T(2,128)S(1)}, u32[]{:S(2)}, u32[]{:S(2)}) %collective-permute-start) | collective-permute-done | bytes 3104 | tf_op jit(solution)/shard_map/ppermute | solution.py:238
  11.1 0.0 collective-permute-done.4.refs_0_
  11.1 0.9 %collective-permute-done.5.refs_1_ = bf16[4,16,256]{2,1,0:T(8,128)(2,1)S(1)} collective-permute-done((bf16[4,16,256]{2,1,0:T(8,128)(2,1)S(1)}, bf16[4,16,256]{2,1,0:T(8,128)(2,1)S(1)}, u32[]{:S(2)}, u32[]{:S(2)}) %collective-permute-start.5) | collective-permute-done | bytes 32800 | tf_op jit(solution)/shard_map/ppermute | solution.py:235
  12.0 0.0 collective-permute-done.6.refs_2_
  12.0 0.1 shard_map.49.refs_3_
  12.0 0.5 %collective-permute-start.7 = (f32[16,256]{1,0:T(8,128)S(1)}, f32[16,256]{1,0:T(8,128)S(1)}, u32[]{:S(2)}, u32[]{:S(2)}) collective-permute-start(f32[16,256]{1,0:T(8,128)S(1)} %shard_map.49.refs_3_), channel_id=1, source_target_pairs={{0,1},{1,0},{2,3},{3,2},{4,5},{5,4},{6,7},{7,6},{8,9},{9,8},{10,11... | collective-permute-start | bytes 49160 | tf_op jit(solution)/shard_map/ppermute | solution.py:238
  12.5 0.0 collective-permute-done.3.next_ref
  12.5 0.2 shard_map.50
  12.7 0.6 %collective-permute-done.7.refs_4_ = f32[16,256]{1,0:T(8,128)S(1)} collective-permute-done((f32[16,256]{1,0:T(8,128)S(1)}, f32[16,256]{1,0:T(8,128)S(1)}, u32[]{:S(2)}, u32[]{:S(2)}) %collective-permute-start.7) | collective-permute-done | bytes 16416 | tf_op jit(solution)/shard_map/ppermute | solution.py:238
  13.3 0.2 shard_map.51
  13.5 2.8 %collective-permute-start.8 = (f32[16,128]{1,0:T(8,128)S(1)}, f32[16,128]{1,0:T(8,128)S(1)}, u32[]{:S(2)}, u32[]{:S(2)}) collective-permute-start(f32[16,128]{1,0:T(8,128)S(1)} %get-tuple-element.39), channel_id=1, source_target_pairs={{0,12},{1,15},{2,14},{3,13},{4,8},{5,11},{6,10},{7,9},{8,4},{9,7},... | collective-permute-start | bytes 24584 | tf_op jit(solution)/shard_map/ppermute | solution.py:235
  16.3 0.0 collective-permute-start.9
  16.3 1.7 %collective-permute-start.10 = (f32[16,128]{1,0:T(8,128)S(1)}, f32[16,128]{1,0:T(8,128)S(1)}, u32[]{:S(2)}, u32[]{:S(2)}) collective-permute-start(f32[16,128]{1,0:T(8,128)S(1)} %get-tuple-element.41), channel_id=1, source_target_pairs={{0,4},{1,7},{2,6},{3,5},{4,0},{5,3},{6,2},{7,1},{8,12},{9,15},{10,... | collective-permute-start | bytes 24584 | tf_op jit(solution)/shard_map/ppermute | solution.py:235
  18.0 1.4 %collective-permute-start.12 = (f32[2,16,128]{2,1,0:T(8,128)S(1)}, f32[2,16,128]{2,1,0:T(8,128)S(1)}, u32[]{:S(2)}, u32[]{:S(2)}) collective-permute-start(f32[2,16,128]{2,1,0:T(8,128)S(1)} %get-tuple-element.42), channel_id=1, source_target_pairs={{0,2},{1,3},{2,0},{3,1},{4,6},{5,7},{6,4},{7,5},{8,10},{9,11},{10,... | collective-permute-start | bytes 49160 | tf_op jit(solution)/shard_map/ppermute | solution.py:235
  19.4 0.0 collective-permute-done.8.refs_0_
  19.4 1.4 %collective-permute-done.9.refs_1_ = f32[16,128]{1,0:T(8,128)S(1)} collective-permute-done((f32[16,128]{1,0:T(8,128)S(1)}, f32[16,128]{1,0:T(8,128)S(1)}, u32[]{:S(2)}, u32[]{:S(2)}) %collective-permute-start.9) | collective-permute-done | bytes 8224 | tf_op jit(solution)/shard_map/ppermute | solution.py:235
  20.8 0.0 collective-permute-done.10.refs_2_
  20.8 0.0 collective-permute-start.11
  20.8 1.2 %collective-permute-done.11.mate_ref = f32[16,128]{1,0:T(8,128)S(1)} collective-permute-done((f32[16,128]{1,0:T(8,128)S(1)}, f32[16,128]{1,0:T(8,128)S(1)}, u32[]{:S(2)}, u32[]{:S(2)}) %collective-permute-start.11) | collective-permute-done | bytes 8224 | tf_op jit(solution)/shard_map/ppermute | solution.py:238
  22.0 0.1 shard_map.53.sums_ref
  22.1 0.0 collective-permute-done.12.got_ref
  22.1 0.8 %shard_map.54 = bf16[2,7,16,256]{3,2,1,0:T(8,128)(2,1)} custom-call(f32[16,128]{1,0:T(8,128)S(1)} %shard_map.53.sums_ref, f32[2,16,128]{2,1,0:T(8,128)S(1)} %collective-permute-done.12.got_ref, bf16[2,7,16,256]{3,2,1,0:T(8,128)(2,1)S(1)} %get-tuple-element.25.own_s.scenes_ref), custom_call_target="tpu_custom_call" | custom-call | tf_op jit(solution)/shard_map/pallas_call | solution.py:308
  (3 shorter events, 0.0 us)
Async XLA Ops:
  0.0 1.9 %collective-permute-start.1 = (bf16[2,7,16,256]{3,2,1,0:T(8,128)(2,1)}, bf16[2,7,16,256]{3,2,1,0:T(8,128)(2,1)S(1)}, u32[]{:S(2)}, u32[]{:S(2)}) collective-permute-start(bf16[2,7,16,256]{3,2,1,0:T(8,128)(2,1)} %bitcast.2), channel_id=1, source_target_pairs={{0,1},{1,0},{2,3},{3,2},{4,5},{5,4},{6,7},{7,6},{8,9},{9,8},{10,11... | collective-permute-start | bytes 344072 | tf_op jit(solution)/shard_map/ppermute | solution.py:238
  0.5 1.4 %collective-permute-start.2 = (bf16[2,16,256]{2,1,0:T(8,128)(2,1)}, bf16[2,16,256]{2,1,0:T(8,128)(2,1)S(1)}, u32[]{:S(2)}, u32[]{:S(2)}) collective-permute-start(bf16[2,16,256]{2,1,0:T(8,128)(2,1)} %refs_1_.1), channel_id=1, source_target_pairs={{0,1},{1,0},{2,3},{3,2},{4,5},{5,4},{6,7},{7,6},{8,9},{9,8},{10,11... | collective-permute-start | bytes 49160 | tf_op jit(solution)/shard_map/ppermute | solution.py:238
  2.0 9.0 %collective-permute-start.4 = (bf16[4,16,256]{2,1,0:T(8,128)(2,1)S(1)}, bf16[4,16,256]{2,1,0:T(8,128)(2,1)S(1)}, u32[]{:S(2)}, u32[]{:S(2)}) collective-permute-start(bf16[4,16,256]{2,1,0:T(8,128)(2,1)S(1)} %get-tuple-element.29), channel_id=1, source_target_pairs={{0,12},{1,11},{2,14},{3,9},{4,8},{5,15},{6,10},{7,13},{8,4},{9,3},... | collective-permute-start | bytes 98312 | tf_op jit(solution)/shard_map/ppermute | solution.py:235
  6.9 5.1 %collective-permute-start.5 = (bf16[4,16,256]{2,1,0:T(8,128)(2,1)S(1)}, bf16[4,16,256]{2,1,0:T(8,128)(2,1)S(1)}, u32[]{:S(2)}, u32[]{:S(2)}) collective-permute-start(bf16[4,16,256]{2,1,0:T(8,128)(2,1)S(1)} %get-tuple-element.30), channel_id=1, source_target_pairs={{0,8},{1,15},{2,10},{3,13},{4,12},{5,11},{6,14},{7,9},{8,0},{9,7},... | collective-permute-start | bytes 98312 | tf_op jit(solution)/shard_map/ppermute | solution.py:235
  6.9 5.1 %collective-permute-start.6 = (bf16[4,16,256]{2,1,0:T(8,128)(2,1)S(1)}, bf16[4,16,256]{2,1,0:T(8,128)(2,1)S(1)}, u32[]{:S(2)}, u32[]{:S(2)}) collective-permute-start(bf16[4,16,256]{2,1,0:T(8,128)(2,1)S(1)} %get-tuple-element.31), channel_id=1, source_target_pairs={{0,4},{1,7},{2,6},{3,5},{4,0},{5,3},{6,2},{7,1},{8,12},{9,15},{10,... | collective-permute-start | bytes 98312 | tf_op jit(solution)/shard_map/ppermute | solution.py:235
  7.5 5.0 %collective-permute-start.3 = (bf16[4,16,256]{2,1,0:T(8,128)(2,1)S(1)}, bf16[4,16,256]{2,1,0:T(8,128)(2,1)S(1)}, u32[]{:S(2)}, u32[]{:S(2)}) collective-permute-start(bf16[4,16,256]{2,1,0:T(8,128)(2,1)S(1)} %get-tuple-element.27), channel_id=1, source_target_pairs={{0,2},{1,3},{2,0},{3,1},{4,6},{5,7},{6,4},{7,5},{8,10},{9,11},{10,... | collective-permute-start | bytes 98312 | tf_op jit(solution)/shard_map/ppermute | solution.py:235
  9.8 1.2 %collective-permute-start = (f32[2,384]{1,0:T(2,128)S(1)}, f32[2,384]{1,0:T(2,128)S(1)}, u32[]{:S(2)}, u32[]{:S(2)}) collective-permute-start(f32[2,384]{1,0:T(2,128)S(1)} %shard_map.47), channel_id=1, source_target_pairs={{0,1},{1,0},{2,3},{3,2},{4,5},{5,4},{6,7},{7,6},{8,9},{9,8},{10,11... | collective-permute-start | bytes 9224 | tf_op jit(solution)/shard_map/ppermute | solution.py:238
  12.0 1.3 %collective-permute-start.7 = (f32[16,256]{1,0:T(8,128)S(1)}, f32[16,256]{1,0:T(8,128)S(1)}, u32[]{:S(2)}, u32[]{:S(2)}) collective-permute-start(f32[16,256]{1,0:T(8,128)S(1)} %shard_map.49.refs_3_), channel_id=1, source_target_pairs={{0,1},{1,0},{2,3},{3,2},{4,5},{5,4},{6,7},{7,6},{8,9},{9,8},{10,11... | collective-permute-start | bytes 49160 | tf_op jit(solution)/shard_map/ppermute | solution.py:238
  13.5 5.9 %collective-permute-start.8 = (f32[16,128]{1,0:T(8,128)S(1)}, f32[16,128]{1,0:T(8,128)S(1)}, u32[]{:S(2)}, u32[]{:S(2)}) collective-permute-start(f32[16,128]{1,0:T(8,128)S(1)} %get-tuple-element.39), channel_id=1, source_target_pairs={{0,12},{1,15},{2,14},{3,13},{4,8},{5,11},{6,10},{7,9},{8,4},{9,7},... | collective-permute-start | bytes 24584 | tf_op jit(solution)/shard_map/ppermute | solution.py:235
  16.3 4.5 %collective-permute-start.9 = (f32[16,128]{1,0:T(8,128)S(1)}, f32[16,128]{1,0:T(8,128)S(1)}, u32[]{:S(2)}, u32[]{:S(2)}) collective-permute-start(f32[16,128]{1,0:T(8,128)S(1)} %get-tuple-element.40), channel_id=1, source_target_pairs={{0,8},{1,11},{2,10},{3,9},{4,12},{5,15},{6,14},{7,13},{8,0},{9,3},... | collective-permute-start | bytes 24584 | tf_op jit(solution)/shard_map/ppermute | solution.py:235
  16.3 4.5 %collective-permute-start.10 = (f32[16,128]{1,0:T(8,128)S(1)}, f32[16,128]{1,0:T(8,128)S(1)}, u32[]{:S(2)}, u32[]{:S(2)}) collective-permute-start(f32[16,128]{1,0:T(8,128)S(1)} %get-tuple-element.41), channel_id=1, source_target_pairs={{0,4},{1,7},{2,6},{3,5},{4,0},{5,3},{6,2},{7,1},{8,12},{9,15},{10,... | collective-permute-start | bytes 24584 | tf_op jit(solution)/shard_map/ppermute | solution.py:235
  18.0 4.1 %collective-permute-start.12 = (f32[2,16,128]{2,1,0:T(8,128)S(1)}, f32[2,16,128]{2,1,0:T(8,128)S(1)}, u32[]{:S(2)}, u32[]{:S(2)}) collective-permute-start(f32[2,16,128]{2,1,0:T(8,128)S(1)} %get-tuple-element.42), channel_id=1, source_target_pairs={{0,2},{1,3},{2,0},{3,1},{4,6},{5,7},{6,4},{7,5},{8,10},{9,11},{10,... | collective-permute-start | bytes 49160 | tf_op jit(solution)/shard_map/ppermute | solution.py:235
  20.8 1.2 %collective-permute-start.11 = (f32[16,128]{1,0:T(8,128)S(1)}, f32[16,128]{1,0:T(8,128)S(1)}, u32[]{:S(2)}, u32[]{:S(2)}) collective-permute-start(f32[16,128]{1,0:T(8,128)S(1)} %shard_map.52.mine_ref), channel_id=1, source_target_pairs={{0,1},{1,0},{2,3},{3,2},{4,5},{5,4},{6,7},{7,6},{8,9},{9,8},{10,11... | collective-permute-start | bytes 24584 | tf_op jit(solution)/shard_map/ppermute | solution.py:238
